TPU v7x, 128 devices: a whole 4x4x4 slice. The times are simulated.
128 devices in a mesh: dp: 16 (over y, x), tensor: 8 (over z, core).
Axes of the slice: x: 4, y: 4, z: 4, core: 2. Of those that a mesh axis runs over, the one named last changes fastest.
Arguments:
- gate_pre: bfloat16 [8192, 14336], P('dp', 'tensor'), may hold values from -6 to 6
- up_pre: bfloat16 [8192, 14336], P('dp', 'tensor'), may hold values from -6 to 6
- out_grad: bfloat16 [8192, 4096], P(('dp', 'tensor')), may hold values from -0.25 to 0.25
- q_start: float32 [8, 4096, 32], P('tensor'), may hold values from -6 to 6
Outputs:
- p_factor: float32 [14336, 32], P('tensor')
- q_factor: float32 [8, 4096, 32], P('tensor')
- new_error: bfloat16 [16, 14336, 4096], P('dp', 'tensor')
All inputs are finite; a program needn't handle non-finite values.
Results may differ from a plain program's by a relative error of at most 0.017.
Values may be sent and summed in bfloat16 or wider, within the bound.
A program may use at most 128 MiB of HBM per device.

v0:
```python
import jax
import jax.numpy as jnp
from jax import lax
from jax.sharding import PartitionSpec as P

epsilon = 1e-06
HIGH = lax.Precision.HIGHEST


def orthonormal(power):
    rank = power.shape[1]
    basis = jnp.zeros(power.shape, jnp.float32)
    for index in range(rank):
        column = power[:, index]
        projection = jnp.dot(basis.T, column, precision=HIGH)
        remainder = column - jnp.dot(basis, projection, precision=HIGH)
        scaled = remainder * lax.rsqrt(jnp.sum(remainder * remainder) + epsilon)
        basis = basis.at[:, index].set(scaled)
    return basis


def on_device(gate_pre, up_pre, out_grad, q_start):
    hidden = (jax.nn.silu(gate_pre.astype(jnp.float32)) * up_pre.astype(jnp.float32)).astype(
        jnp.bfloat16
    )
    q_local = q_start[0]
    replicas = lax.axis_size("dp")
    full_grad = lax.all_gather(out_grad, "tensor", axis=0, tiled=True)
    gradient = lax.dot_general(
        hidden, full_grad, (((0,), (0,)), ((), ())), preferred_element_type=jnp.float32
    )
    p_part = jnp.dot(gradient, q_local, precision=HIGH)
    p_sum = lax.psum(p_part, "dp")
    basis = orthonormal(p_sum)
    q_part = lax.dot_general(
        gradient,
        basis,
        (((0,), (0,)), ((), ())),
        precision=HIGH,
        preferred_element_type=jnp.float32,
    )
    q_mean = lax.psum(q_part.astype(jnp.bfloat16), "dp").astype(jnp.float32) / replicas
    new_error = (gradient - jnp.dot(basis, q_mean.T, precision=HIGH)).astype(jnp.bfloat16)
    return (basis, q_mean[None], new_error[None])


def solution(mesh):
    placed = (
        P("dp", "tensor"),
        P("dp", "tensor"),
        P(("dp", "tensor"), None),
        P("tensor", None, None),
    )
    return jax.shard_map(
        on_device,
        mesh=mesh,
        in_specs=placed,
        out_specs=(P("tensor", None), P("tensor", None, None), P("dp", "tensor", None)),
        check_vma=False,
    )
```

profile of v0, /device:TPU:1, one launch (start us, length us, event | category | flops | bytes accessed | tf_op | source)
XLA Modules:
  0.0 412.1 jit_solution(18178569757727743683)
XLA Ops:
  7.2 0.7 all-gather.2.cloned.1.call-update
  8.0 37.8 %all-gather.2.cloned.1.call-done = bf16[512,4096]{1,0:T(8,128)(2,1)} async-done(((bf16[64,4096]{1,0:T(8,128)(2,1)}), bf16[512,4096]{1,0:T(8,128)(2,1)}) %all-gather.2.cloned.1.call-update) | async-done | bytes 4194320 | tf_op jit(solution)/shard_map/all_gather | solution.py:28
  45.7 16.5 %fusion.6 = f32[1792,4096]{1,0:T(8,128)} fusion(bf16[512,4096]{1,0:T(8,128)(2,1)} %all-gather.2.cloned.1.call-done, bf16[512,1792]{1,0:T(8,128)(2,1)} %param.69, bf16[512,1792]{1,0:T(8,128)(2,1)} %param.68), kind=kOutput, calls=%fused_computation.10 | convolution fusion | flops 7523532800 | bytes 37224448 | tf_op jit(solution)/shard_map/dot_general | solution.py:29
  62.2 30.6 %fusion.11 = f32[1792,32]{0,1:T(8,128)} fusion(f32[1792,4096]{1,0:T(8,128)} %fusion.6, f32[1,4096,32]{1,2,0:T(8,128)S(1)} %copy-done), kind=kOutput, calls=%fused_computation.77 | convolution fusion | flops 2818572288 | bytes 30113792 | tf_op jit(solution)/shard_map/dot_general | solution.py:32
  93.1 0.6 compare_reduce_fusion.30
  93.7 0.6 compare_reduce_fusion.29
  94.3 0.7 compare_reduce_fusion.28
  95.1 0.7 compare_reduce_fusion.27
  95.8 0.7 compare_reduce_fusion.26
  96.5 0.7 compare_reduce_fusion.25
  97.1 0.7 compare_reduce_fusion.24
  97.8 0.6 compare_reduce_fusion.23
  98.4 0.7 compare_reduce_fusion.22
  99.1 0.6 compare_reduce_fusion.21
  99.7 0.7 compare_reduce_fusion.20
  100.4 0.7 compare_reduce_fusion.19
  101.2 0.7 compare_reduce_fusion.18
  101.9 0.7 compare_reduce_fusion.17
  102.6 0.6 compare_reduce_fusion.16
  103.2 0.7 compare_reduce_fusion.15
  103.9 0.7 compare_reduce_fusion.14
  104.6 0.6 compare_reduce_fusion.13
  105.3 0.7 compare_reduce_fusion.12
  105.9 0.7 compare_reduce_fusion.11
  106.6 0.7 compare_reduce_fusion.10
  107.9 0.7 compare_reduce_fusion.8
  108.6 0.6 compare_reduce_fusion.7
  109.3 0.7 compare_reduce_fusion.6
  110.0 0.7 compare_reduce_fusion.5
  110.6 0.6 compare_reduce_fusion.4
  111.3 0.7 compare_reduce_fusion.3
  112.0 0.7 compare_reduce_fusion.2
  112.6 0.6 compare_reduce_fusion.1
  113.3 0.7 compare_reduce_fusion
  114.0 60.5 %all-reduce.4.cloned.1.call-done = f32[1792,32]{0,1:T(8,128)} async-done(((f32[1792,32]{0,1:T(8,128)}), f32[1792,32]{0,1:T(8,128)}) %all-reduce.4.cloned.1.call-update) | async-done | bytes 229392 | tf_op jit(solution)/shard_map/psum | solution.py:33
  174.5 1.8 fusion.10
  176.3 0.7 broadcast_reduce_fusion
  177.0 1.6 slice_reduce_fusion.19
  179.9 0.7 multiply_select_fusion.1
  180.6 1.0 convolution_bitcast_fusion.30
  183.1 0.7 multiply_select_fusion
  184.0 1.0 convolution_bitcast_fusion.29
  186.7 0.7 broadcast_select_fusion.28
  187.6 1.0 convolution_bitcast_fusion.28
  190.3 0.7 broadcast_select_fusion.27
  191.2 1.0 convolution_bitcast_fusion.27
  193.9 0.6 broadcast_select_fusion.26
  194.7 1.0 convolution_bitcast_fusion.26
  197.4 0.6 broadcast_select_fusion.25
  198.2 1.0 convolution_bitcast_fusion.25
  200.9 0.6 broadcast_select_fusion.24
  201.7 1.0 convolution_bitcast_fusion.24
  212.5 0.6 broadcast_select_fusion.20
  215.2 0.7 broadcast_select_fusion.19
  221.0 0.7 broadcast_select_fusion.17
  226.4 0.7 broadcast_select_fusion.15
  229.2 0.6 broadcast_select_fusion.14
  237.2 0.7 broadcast_select_fusion.11
  240.0 0.6 broadcast_select_fusion.10
  245.3 0.7 broadcast_select_fusion.8
  269.9 21.3 %convolution_convert_fusion = bf16[4096,32]{0,1:T(8,128)(2,1)} fusion(f32[1792,4096]{1,0:T(8,128)} %fusion.6, f32[1792,32]{0,1:T(8,128)S(1)} %scatter.159), kind=kOutput, calls=%fused_computation.4 | convolution fusion | flops 2818703360 | bytes 29851648 | tf_op jit(solution)/shard_map/dot_general | solution.py:35
  291.3 83.6 %all-reduce.6.cloned.1.call-done = bf16[4096,32]{0,1:T(8,128)(2,1)} async-done(((bf16[4096,32]{0,1:T(8,128)(2,1)}), bf16[4096,32]{0,1:T(8,128)(2,1)}) %all-reduce.6.cloned.1.call-update) | async-done | bytes 262160 | tf_op jit(solution)/shard_map/psum | solution.py:42
  374.9 29.8 %fusion = bf16[1,1792,4096]{2,1,0:T(8,128)(2,1)} fusion(f32[1792,4096]{1,0:T(8,128)} %fusion.6, f32[1792,32]{0,1:T(8,128)S(1)} %scatter.159, bf16[4096,32]{0,1:T(8,128)(2,1)} %all-reduce.6.cloned.1.call-done), kind=kOutput, calls=%fused_computation.1 | convolution fusion | flops 2833514496 | bytes 44531712 | tf_op jit(solution)/shard_map/dot_general | solution.py:43
  404.7 0.8 fusion.13
  (183 shorter events, 51.8 us)
Async XLA Ops:
  7.2 55.0 %copy-start = (f32[1,4096,32]{1,2,0:T(8,128)S(1)}, f32[1,4096,32]{1,2,0:T(8,128)}, u32[]{:S(2)}) copy-start(f32[1,4096,32]{1,2,0:T(8,128)} %param.71) | copy-start | bytes 1572868
  7.2 38.5 %all-gather.2.cloned.1.call-start = ((), (), s32[]{:S(2)}) async-start(), calls=%async_computation | async-start | bytes 4718592 | tf_op jit(solution)/shard_map/all_gather | solution.py:28
  7.9 166.6 %all-reduce.4.cloned.1.call-start = ((), (), s32[]{:S(2)}) async-start(), calls=%async_computation.1 | async-start | bytes 458752 | tf_op jit(solution)/shard_map/psum | solution.py:33
  92.8 282.1 %all-reduce.6.cloned.1.call-start = ((), (), s32[]{:S(2)}) async-start(), calls=%async_computation.2 | async-start | bytes 524288 | tf_op jit(solution)/shard_map/psum | solution.py:42
  174.5 30.7 %copy-start.2 = (f32[1792,32]{0,1:T(8,128)S(1)}, f32[1792,32]{0,1:T(8,128)}, u32[]{:S(2)}) copy-start(f32[1792,32]{0,1:T(8,128)} %all-reduce.4.cloned.1.call-done) | copy-start | bytes 688132
  269.9 105.0 %copy-start.1 = (f32[1792,32]{0,1:T(8,128)}, f32[1792,32]{0,1:T(8,128)S(1)}, u32[]{:S(2)}) copy-start(f32[1792,32]{0,1:T(8,128)S(1)} %scatter.159) | copy-start | bytes 688132
  374.9 29.8 %copy-start.3 = (bf16[4096,32]{0,1:T(8,128)(2,1)S(1)}, bf16[4096,32]{0,1:T(8,128)(2,1)}, u32[]{:S(2)}) copy-start(bf16[4096,32]{0,1:T(8,128)(2,1)} %all-reduce.6.cloned.1.call-done) | copy-start | bytes 786436
Sparse Core Ops, SparseCore 0:
  9.7 35.9 all-gather.1
  92.9 81.5 all-reduce.3
  291.4 83.4 all-reduce.5
where the time goes:
time: 414 us; the launch traced here: 412 us
  waiting for transfers between devices  183 us (44%)
  matrix products  123 us (30%)
  other arithmetic  61 us (15%)
  between operations  36.9 us (9%)
  local copies, waits for them, and re-layouts  8.52 us (2%)
    psum x1, waiting for transfers between devices, on_device(): lax.psum(q_part.astype(jnp.bfloat16), 'dp').astype(jnp.float32) / replicas  83.6 us
    psum x1, waiting for transfers between devices, on_device(): p_sum = lax.psum(p_part, 'dp')  60.5 us
    another operation x62, other arithmetic  40.8 us
    all_gather x1, waiting for transfers between devices, on_device(): full_grad = lax.all_gather(out_grad, 'tensor', axis=0, tiled=True)  37.8 us
    dot_general x1, matrix products, on_device(): p_part = jnp.dot(gradient, q_local, precision=HIGH)  30.6 us
    dot_general x1, matrix products, on_device(): jnp.dot(basis, q_mean.T, precision=HIGH)  29.8 us
    dot_general x1, matrix products, on_device(): lax.dot_general(gradient, basis, (((0,), (0,)), ((), ())), precision=HIGH...  21.3 us
    reduce_sum x32, other arithmetic, orthonormal(): scaled = remainder * lax.rsqrt(jnp.sum(remainder * remainder) + epsilon)  19.3 us
  transfers between devices with their start and end apart: 3, of which 3 were waited for; matrix products, arithmetic and copies ran while one was open for 5% of the time, Pallas kernels for 0%

commit v1 on v0

v1 whole, which is shorter than its diff:
```python
import functools

import jax
import jax.numpy as jnp
from jax import lax
from jax.experimental import pallas as pl
from jax.experimental.pallas import tpu as pltpu
from jax.sharding import PartitionSpec as P

EPSILON = 1e-06
HIGH = lax.Precision.HIGHEST
BF16 = jnp.bfloat16
F32 = jnp.float32
MESH = pl.DeviceIdType.MESH

TOK = 512
ROWS = 64
D = 4096
FF = 1792
RANK = 32
CHUNKS = 8
WIDTH = D // CHUNKS
DP = 16
AHEAD = 3
PSLICE = 128
PSLICES = FF // PSLICE
QSLICE = D // DP
TILE = 256


def dot(a, b, contract):
    return lax.dot_general(a, b, ((contract[:1], contract[1:]), ((), ())), preferred_element_type=F32)


def split2(x):
    high = x.astype(BF16)
    low = (x - high.astype(F32)).astype(BF16)
    return jnp.concatenate([high, low], axis=0)


def join2(x):
    return x[:RANK] + x[RANK:]


def gram_schmidt(gram, coeff_ref):
    y = gram
    rows = lax.broadcasted_iota(jnp.int32, (RANK, RANK), 0)
    cols = lax.broadcasted_iota(jnp.int32, (RANK, RANK), 1)
    u = jnp.where(rows == cols, 1.0, 0.0).astype(F32)
    for j in range(RANK):
        y_row = y[j : j + 1, :]
        u_row = u[j : j + 1, :]
        norm = jnp.sum(y_row * u_row, axis=1, keepdims=True)
        scale = lax.rsqrt(jnp.maximum(norm, 0.0) + EPSILON)
        coeff_ref[j : j + 1, :] = u_row * scale
        if j < RANK - 1:
            factor = y[:, j : j + 1] * (scale * scale)
            y = y - factor * y_row
            u = u - factor * u_row


def exchange_kernel(
    gate_hbm, up_hbm, out_grad_hbm, q_hbm,
    grad_ref, p_ref, q_ref,
    g_buf, gate_buf, up_buf, h_buf, ht_buf, q_buf, qs_buf, proj, coeff,
    p_part, p_in, p_all, q_part, q_in, q_all,
    local_sem, sem_up_s, sem_up_r, sem_dn_s, sem_dn_r, sem_fu_s, sem_fu_r, sem_fd_s, sem_fd_r,
    sem_sib_s, sem_sib_r, sem_ar_s, sem_ar_r,
):
    dp = lax.axis_index("dp")
    tensor = lax.axis_index("tensor")
    z = tensor // 2
    core = tensor % 2
    t_up = lax.rem(z + 1, 4) * 2 + core
    t_dn = lax.rem(z + 3, 4) * 2 + core
    t_far = lax.rem(z + 2, 4) * 2 + core
    t_sib = z * 2 + 1 - core

    def rows_of(t):
        return pl.ds(pl.multiple_of(t * ROWS, ROWS), ROWS)

    def local_g(c):
        return pltpu.make_async_copy(
            out_grad_hbm.at[:, pl.ds(pl.multiple_of(c * WIDTH, WIDTH), WIDTH)],
            g_buf.at[c, rows_of(tensor), :], local_sem.at[c])

    def local_in(k):
        src, dst = ((gate_hbm, gate_buf), (up_hbm, up_buf), (q_hbm, q_buf))[k]
        return pltpu.make_async_copy(src, dst, local_sem.at[CHUNKS + k])

    for c in range(CHUNKS):
        local_g(c).start()
    for k in range(3):
        local_in(k).start()

    barrier = pltpu.get_barrier_semaphore()
    for t in (t_up, t_dn, t_sib):
        pl.semaphore_signal(barrier, inc=1, device_id={"tensor": t}, device_id_type=MESH)

    def greet(k, carry):
        pl.semaphore_signal(
            barrier, inc=1, device_id={"dp": lax.rem(dp + k, DP)}, device_id_type=MESH)
        return carry

    lax.fori_loop(1, DP, greet, 0)
    pl.semaphore_wait(barrier, 3 + DP - 1)

    def remote(c, rows, t, send, recv):
        ref = g_buf.at[c, rows, :]
        return pltpu.make_async_remote_copy(
            src_ref=ref, dst_ref=ref, send_sem=send, recv_sem=recv,
            device_id={"tensor": t}, device_id_type=MESH)

    half = ROWS // 2

    def first_half(t):
        return pl.ds(pl.multiple_of(t * ROWS, half), half)

    def last_half(t):
        return pl.ds(pl.multiple_of(t * ROWS + half, half), half)

    def send_up(c):
        return remote(c, rows_of(tensor), t_up, sem_up_s.at[c], sem_up_r.at[c])

    def send_dn(c):
        return remote(c, rows_of(tensor), t_dn, sem_dn_s.at[c], sem_dn_r.at[c])

    def forward_up(c):
        return remote(c, first_half(t_dn), t_up, sem_fu_s.at[c], sem_fu_r.at[c])

    def forward_dn(c):
        return remote(c, last_half(t_up), t_dn, sem_fd_s.at[c], sem_fd_r.at[c])

    def send_sib(c, t, k):
        return remote(c, rows_of(t), t_sib, sem_sib_s.at[c, k], sem_sib_r.at[c, k])

    def start_own(c):
        local_g(c).wait()
        send_up(c).start()
        send_dn(c).start()
        send_sib(c, tensor, 0).start()

    def middle(c):
        remote(c, rows_of(t_dn), t_up, sem_up_s.at[c], sem_up_r.at[c]).wait_recv()
        forward_up(c).start()
        send_sib(c, t_dn, 1).start()
        remote(c, rows_of(t_up), t_dn, sem_dn_s.at[c], sem_dn_r.at[c]).wait_recv()
        forward_dn(c).start()
        send_sib(c, t_up, 2).start()

    def last(c):
        remote(c, first_half(t_far), t_up, sem_fu_s.at[c], sem_fu_r.at[c]).wait_recv()
        remote(c, last_half(t_far), t_dn, sem_fd_s.at[c], sem_fd_r.at[c]).wait_recv()
        send_sib(c, t_far, 3).start()

    def arrived(c):
        for k in range(4):
            send_sib(c, tensor, k).wait_recv()

    for c in range(AHEAD):
        start_own(c)

    local_in(0).wait()
    local_in(1).wait()

    def make_hidden(i, carry):
        rows = pl.ds(pl.multiple_of(i * 64, 64), 64)
        v = gate_buf[rows, :].astype(F32)
        w = up_buf[rows, :].astype(F32)
        h_buf[rows, :] = ((0.5 * v) * (1.0 + jnp.tanh(0.5 * v)) * w).astype(BF16)
        return carry

    lax.fori_loop(0, TOK // 64, make_hidden, 0)

    def turn_hidden(i, carry):
        cols = pl.ds(pl.multiple_of(i * TILE, TILE), TILE)
        ht_buf[cols, :] = h_buf[:, cols].T
        return carry

    lax.fori_loop(0, FF // TILE, turn_hidden, 0)
    local_in(2).wait()
    qs_buf[...] = split2(q_buf[...])
    proj[...] = jnp.zeros_like(proj)

    def gather_step(i, carry):
        @pl.when(i + AHEAD < CHUNKS)
        def _():
            start_own(i + AHEAD)

        @pl.when(i < CHUNKS)
        def _():
            middle(i)

        @pl.when(jnp.logical_and(i >= 1, i <= CHUNKS))
        def _():
            last(i - 1)

        @pl.when(i >= 2)
        def _():
            c = i - 2
            arrived(c)
            cols = pl.ds(pl.multiple_of(c * WIDTH, WIDTH), WIDTH)
            proj[...] += dot(qs_buf[:, cols], g_buf[c], (1, 1))

            def grad_tile(m, carry):
                rows = pl.ds(pl.multiple_of(m * TILE, TILE), TILE)
                grad_ref[rows, cols] = dot(ht_buf[rows, :], g_buf[c], (1, 0))
                return carry

            lax.fori_loop(0, FF // TILE, grad_tile, 0)

        return carry

    lax.fori_loop(0, CHUNKS + 2, gather_step, 0)

    projected = split2(join2(proj[...]))
    power = join2(dot(projected, h_buf[...], (1, 0)))
    for s in range(DP):
        if s < PSLICES:
            p_part[s] = power[:, s * PSLICE : (s + 1) * PSLICE]
        else:
            p_part[s] = jnp.zeros((RANK, PSLICE), F32)

    def all_reduce(part, landing, total, sums, k0):
        def scatter(k):
            peer = lax.rem(dp + k, DP)
            return pltpu.make_async_remote_copy(
                src_ref=part.at[peer], dst_ref=landing.at[dp],
                send_sem=sem_ar_s.at[k0], recv_sem=sem_ar_r.at[k0],
                device_id={"dp": peer}, device_id_type=MESH)

        def gather(k):
            peer = lax.rem(dp + k, DP)
            return pltpu.make_async_remote_copy(
                src_ref=total.at[dp], dst_ref=total.at[dp],
                send_sem=sem_ar_s.at[k0 + 1], recv_sem=sem_ar_r.at[k0 + 1],
                device_id={"dp": peer}, device_id_type=MESH)

        def start(copy):
            def body(k, carry):
                copy(k).start()
                return carry

            lax.fori_loop(1, DP, body, 0)

        def wait_all(ref, sem):
            pltpu.make_async_copy(ref.at[pl.ds(0, DP - 1)], ref.at[pl.ds(0, DP - 1)], sem).wait()

        start(scatter)
        landing[dp] = part[dp]
        wait_all(landing, sem_ar_r.at[k0])
        total[dp] = sums(landing)
        start(gather)
        wait_all(total, sem_ar_r.at[k0 + 1])
        wait_all(part, sem_ar_s.at[k0])
        wait_all(total, sem_ar_s.at[k0 + 1])

    def sum_p(landing):
        value = landing[0]
        for s in range(1, DP):
            value = value + landing[s]
        return value

    def sum_q(landing):
        value = landing[0].astype(F32)
        for s in range(1, DP):
            value = value + landing[s].astype(F32)
        return (value * (1.0 / DP)).astype(BF16)

    all_reduce(p_part, p_in, p_all, sum_p, 0)
    power = jnp.concatenate([p_all[s] for s in range(PSLICES)], axis=1)
    gram = lax.dot_general(
        power, power, (((1,), (1,)), ((), ())), precision=HIGH, preferred_element_type=F32)
    gram_schmidt(gram, coeff)
    basis = jnp.dot(coeff[...], power, precision=HIGH, preferred_element_type=F32)
    p_ref[...] = basis

    mapped = split2(join2(dot(split2(basis), ht_buf[...], (1, 0))))
    for c in range(CHUNKS):
        terms = join2(dot(mapped, g_buf[c], (1, 0))).astype(BF16)
        for k in range(WIDTH // QSLICE):
            q_part[c * (WIDTH // QSLICE) + k] = terms[:, k * QSLICE : (k + 1) * QSLICE]
    all_reduce(q_part, q_in, q_all, sum_q, 2)
    for s in range(DP):
        q_ref[:, s * QSLICE : (s + 1) * QSLICE] = q_all[s].astype(F32)

    def drain(c, carry):
        send_up(c).wait_send()
        send_dn(c).wait_send()
        forward_up(c).wait_send()
        forward_dn(c).wait_send()
        for k in range(4):
            send_sib(c, tensor, k).wait_send()
        return carry

    lax.fori_loop(0, CHUNKS, drain, 0)


ROW_TILE = 128


def error_kernel(grad_ref, p_ref, q_ref, p_out, q_out, error_ref, q2):
    step = pl.program_id(0)

    @pl.when(step == 0)
    def _():
        p_out[...] = p_ref[...]
        q_out[...] = q_ref[...]
        q_once = q_ref[...].astype(BF16)
        q2[...] = jnp.concatenate([q_once, q_once], axis=0)

    rows = pl.ds(pl.multiple_of(step * ROW_TILE, ROW_TILE), ROW_TILE)
    p2 = split2(p_ref[:, rows])
    for k in range(4):
        cols = pl.ds(k * (D // 4), D // 4)
        low_rank = dot(p2, q2[:, cols], (0, 0))
        error_ref[:, cols] = (grad_ref[rows, cols] - low_rank).astype(BF16)


def on_device(gate_pre, up_pre, out_grad, q_start):
    q_turned = q_start[0].T
    any_space = pl.BlockSpec(memory_space=pl.ANY)
    vmem_space = pl.BlockSpec(memory_space=pltpu.VMEM)
    dma = pltpu.SemaphoreType.DMA
    grad, p_turned, q_mean = pl.pallas_call(
        exchange_kernel,
        out_shape=(
            pltpu.VMEM((FF, D), F32),
            pltpu.VMEM((RANK, FF), F32),
            pltpu.VMEM((RANK, D), F32),
        ),
        in_specs=[any_space] * 4,
        out_specs=(vmem_space,) * 3,
        scratch_shapes=[
            pltpu.VMEM((CHUNKS, TOK, WIDTH), BF16),
            pltpu.VMEM((TOK, FF), BF16),
            pltpu.VMEM((TOK, FF), BF16),
            pltpu.VMEM((TOK, FF), BF16),
            pltpu.VMEM((FF, TOK), BF16),
            pltpu.VMEM((RANK, D), F32),
            pltpu.VMEM((2 * RANK, D), BF16),
            pltpu.VMEM((2 * RANK, TOK), F32),
            pltpu.VMEM((RANK, RANK), F32),
            pltpu.VMEM((DP, RANK, PSLICE), F32),
            pltpu.VMEM((DP, RANK, PSLICE), F32),
            pltpu.VMEM((DP, RANK, PSLICE), F32),
            pltpu.VMEM((DP, RANK, QSLICE), BF16),
            pltpu.VMEM((DP, RANK, QSLICE), BF16),
            pltpu.VMEM((DP, RANK, QSLICE), BF16),
            dma((CHUNKS + 3,)),
            dma((CHUNKS,)), dma((CHUNKS,)), dma((CHUNKS,)), dma((CHUNKS,)),
            dma((CHUNKS,)), dma((CHUNKS,)), dma((CHUNKS,)), dma((CHUNKS,)),
            dma((CHUNKS, 4)), dma((CHUNKS, 4)), dma((4,)), dma((4,)),
        ],
        compiler_params=pltpu.CompilerParams(
            collective_id=0, has_side_effects=True, vmem_limit_bytes=24 * 2**20),
        name="exchange",
    )(*[pltpu.with_memory_space_constraint(v, pltpu.HBM) for v in (gate_pre, up_pre, out_grad, q_turned)])
    p_out, q_out, new_error = pl.pallas_call(
        error_kernel,
        grid=(FF // ROW_TILE,),
        out_shape=(
            jax.ShapeDtypeStruct((RANK, FF), F32),
            jax.ShapeDtypeStruct((RANK, D), F32),
            jax.ShapeDtypeStruct((FF, D), BF16),
        ),
        in_specs=[vmem_space] * 3,
        out_specs=(
            pl.BlockSpec((RANK, FF), lambda i: (0, 0)),
            pl.BlockSpec((RANK, D), lambda i: (0, 0)),
            pl.BlockSpec((ROW_TILE, D), lambda i: (i, 0)),
        ),
        scratch_shapes=[pltpu.VMEM((2 * RANK, D), BF16)],
        compiler_params=pltpu.CompilerParams(vmem_limit_bytes=24 * 2**20),
        name="error",
    )(grad, p_turned, q_mean)
    return (p_out.T, q_out.T[None], new_error[None])


def solution(mesh):
    placed = (
        P("dp", "tensor"),
        P("dp", "tensor"),
        P(("dp", "tensor"), None),
        P("tensor", None, None),
    )
    return jax.shard_map(
        on_device,
        mesh=mesh,
        in_specs=placed,
        out_specs=(P("tensor", None), P("tensor", None, None), P("dp", "tensor", None)),
        check_vma=False,
    )
```

time: 414 us -> 85 us (0.21)
  the two profiles are of different devices: /device:TPU:1 before, /device:TPU:0 now
where the time goes in v1:
time: 85 us; the launch traced here: 84.9 us
  Pallas kernels  84.3 us (99%)
    pallas_call x1, Pallas kernels, on_device(): pl.pallas_call(exchange_kernel, out_shape=(pltpu.VMEM((FF, D), F32), pltp...  73.5 us
    pallas_call x1, Pallas kernels, on_device(): pl.pallas_call(error_kernel, grid=(FF // ROW_TILE,), out_shape=(jax.Shape...  10.7 us

profile of v1, /device:TPU:0, one launch (start us, length us, event | category | flops | bytes accessed | tf_op | source)
XLA Modules:
  0.0 84.9 jit_solution(9885354998978805544)
XLA Ops:
  0.6 73.5 %exchange.1 = (f32[1792,4096]{1,0:T(8,128)S(1)}, f32[32,1792]{1,0:T(8,128)S(1)}, f32[32,4096]{1,0:T(8,128)S(1)}) custom-call(bf16[512,1792]{1,0:T(8,128)(2,1)} %gate_hbm.1, bf16[512,1792]{1,0:T(8,128)(2,1)} %up_hbm.1, bf16[64,4096]{1,0:T(8,128)(2,1)} %out_grad_hbm.1, f32[32,4096]{1,0:T(8,128)} %bitcast.8), custom_call_target="tpu_custom_call" | custom-call | tf_op jit(solution)/shard_map/exchange/pallas_call | solution.py:325
  74.2 10.7 %error.1 = (f32[32,1792]{1,0:T(8,128)}, f32[32,4096]{1,0:T(8,128)}, bf16[1792,4096]{1,0:T(8,128)(2,1)}) custom-call(f32[1792,4096]{1,0:T(8,128)S(1)} %get-tuple-element.9.grad_ref, f32[32,1792]{1,0:T(8,128)S(1)} %get-tuple-element.10.p_ref, f32[32,4096]{1,0:T(8,128)S(1)} %get-tuple-element.11.q_ref), custom_call_target="tpu_custom_call" | custom-call | tf_op jit(solution)/shard_map/error/pallas_call | solution.py:359

commit v2 on v0

v2 whole, which is shorter than its diff:
```python
import functools

import jax
import jax.numpy as jnp
from jax import lax
from jax.experimental import pallas as pl
from jax.experimental.pallas import tpu as pltpu
from jax.sharding import PartitionSpec as P

EPSILON = 1e-06
HIGH = lax.Precision.HIGHEST
BF16 = jnp.bfloat16
F32 = jnp.float32
MESH = pl.DeviceIdType.MESH

TOK = 512
ROWS = 64
D = 4096
FF = 1792
RANK = 32
HALF = ROWS // 2
CHIP = 2 * ROWS
DP = 16
PSLICE = 128
PSLICES = FF // PSLICE
QSLICE = D // DP
TILE = 256
WIDTH = 512
GRAD_TILE = 448
BLOCK = 4
ERROR_TILE = 128
ERROR_WIDTH = 256
VMEM_BYTES = 24 * 2**20


def dot(a, b, contract):
    return lax.dot_general(a, b, ((contract[:1], contract[1:]), ((), ())), preferred_element_type=F32)


def split2(x):
    high = x.astype(BF16)
    low = (x - high.astype(F32)).astype(BF16)
    return jnp.concatenate([high, low], axis=0)


def join2(x):
    return x[:RANK] + x[RANK:]


def gram_schmidt(gram, coeff_ref):
    rows = lax.broadcasted_iota(jnp.int32, (RANK, RANK), 0)
    cols = lax.broadcasted_iota(jnp.int32, (RANK, RANK), 1)
    y = gram
    u = jnp.where(rows == cols, 1.0, 0.0).astype(F32)
    base = 0

    def spread_row(m, r):
        return jnp.broadcast_to(m[r : r + 1, :], (8, RANK))

    def tall(m, n):
        return jnp.concatenate([m] * (n // 8), axis=0) if n > 8 else m

    for j in range(0, RANK, BLOCK):
        at = j - base
        left = RANK - base
        y_row = [spread_row(y, at + a) for a in range(BLOCK)]
        u_row = [spread_row(u, at + a) for a in range(BLOCK)]
        y_col = [jnp.broadcast_to(y[:, j + a : j + a + 1], (left, RANK)) for a in range(BLOCK)]
        pairs = [(a, c) for a in range(BLOCK) for c in range(a, BLOCK)]
        x = {
            (a, c): jnp.broadcast_to(
                jnp.sum(u_row[a] * y_row[c], axis=1, keepdims=True), (8, RANK))
            for a, c in pairs
        }
        v = {(a, c): spread_row(y_col[a], at + c) for a, c in pairs if c > a}
        inverse = []
        for a in range(BLOCK):
            norm = x[a, a]
            scale = lax.rsqrt(jnp.maximum(norm, 0.0) + EPSILON)
            inverse.append(scale * scale)
            coeff_ref[j + a : j + a + 1, :] = (u_row[a] * scale)[:1]
            f = {c: v[a, c] * inverse[a] for c in range(a + 1, BLOCK)}
            for c in range(a + 1, BLOCK):
                for d in range(c, BLOCK):
                    x[c, d] = x[c, d] - f[c] * x[a, d] - f[d] * (x[a, c] - norm * f[c])
                    if d > c:
                        v[c, d] = v[c, d] - f[c] * v[a, d]
                y_row[c] = y_row[c] - f[c] * y_row[a]
                u_row[c] = u_row[c] - f[c] * u_row[a]
                y_col[c] = y_col[c] - tall(f[c], left) * y_col[a]
        if j + BLOCK < RANK:
            for a in range(BLOCK):
                y = y - y_col[a] * tall(inverse[a] * y_row[a], left)
                u = u - y_col[a] * tall(inverse[a] * u_row[a], left)
            if (j + BLOCK) % 8 == 0:
                y = y[j + BLOCK - base :, :]
                u = u[j + BLOCK - base :, :]
                base = j + BLOCK


def exchange_kernel(
    gate_hbm, up_hbm, out_grad_hbm, q_hbm,
    grad_ref, p_ref, q_ref, p_turned_ref,
    g_buf, gate_buf, up_buf, h_buf, ht_buf, q_buf, qs_buf, proj, coeff,
    p_part, p_in, p_all, q_part, q_in, q_all,
    local_sem, own_s, own_r, far_s, far_r, sib_s, sib_r, sum_s, sum_r,
):
    dp = lax.axis_index("dp")
    tensor = lax.axis_index("tensor")
    z = tensor // 2
    core = lax.rem(tensor, 2)
    z_up, z_far, z_dn = lax.rem(z + 1, 4), lax.rem(z + 2, 4), lax.rem(z + 3, 4)
    t_up, t_far, t_dn = z_up * 2 + core, z_far * 2 + core, z_dn * 2 + core
    t_sib = z * 2 + 1 - core
    y = dp // 4
    x = lax.rem(dp, 4)
    offsets = sorted(
        ((a, b) for a in range(4) for b in range(4) if a or b),
        key=lambda o: -(min(o[0], 4 - o[0]) + min(o[1], 4 - o[1])),
    )
    peers = [lax.rem(y + a, 4) * 4 + lax.rem(x + b, 4) for a, b in offsets]

    def half_of(t, h):
        return pl.ds(pl.multiple_of(t * ROWS + h * HALF, HALF), HALF)

    def local_g(h):
        return pltpu.make_async_copy(
            out_grad_hbm.at[pl.ds(h * HALF, HALF), :], g_buf.at[half_of(tensor, h), :],
            local_sem.at[h])

    def local_in(k):
        src, dst = ((gate_hbm, gate_buf), (up_hbm, up_buf), (q_hbm, q_buf))[k]
        return pltpu.make_async_copy(src, dst, local_sem.at[2 + k])

    barrier = pltpu.get_barrier_semaphore()
    for t in (t_up, t_dn, t_sib):
        pl.semaphore_signal(barrier, inc=1, device_id={"tensor": t}, device_id_type=MESH)
    for peer in peers:
        pl.semaphore_signal(barrier, inc=1, device_id={"dp": peer}, device_id_type=MESH)
    for h in range(2):
        local_g(h).start()
    for k in range(3):
        local_in(k).start()
    pl.semaphore_wait(barrier, 3 + DP - 1)

    def piece(t, h, to, send, recv):
        ref = g_buf.at[half_of(t, h), :]
        return pltpu.make_async_remote_copy(
            src_ref=ref, dst_ref=ref, send_sem=send, recv_sem=recv,
            device_id={"tensor": to}, device_id_type=MESH)

    def own(way, k):
        h = k if way == 0 else 1 - k
        return piece(tensor, h, (t_up, t_dn)[way], own_s.at[way, k], own_r.at[way, k])

    def onward(way):
        return piece((t_dn, t_up)[way], way, (t_up, t_dn)[way], far_s.at[way], far_r.at[way])

    def across(n, t, h):
        return piece(t, h, t_sib, sib_s.at[n], sib_r.at[n])

    for h in range(2):
        local_g(h).wait()
    for k in range(2):
        for way in range(2):
            own(way, k).start()
    for h in range(2):
        across(h, tensor, h).start()

    local_in(0).wait()
    local_in(1).wait()

    def make_hidden(i, carry):
        rows = pl.ds(pl.multiple_of(i * 64, 64), 64)
        v = gate_buf[rows, :].astype(F32)
        w = up_buf[rows, :].astype(F32)
        h_buf[rows, :] = ((0.5 * v) * (1.0 + jnp.tanh(0.5 * v)) * w).astype(BF16)
        return carry

    lax.fori_loop(0, TOK // 64, make_hidden, 0)

    def turn_hidden(i, carry):
        cols = pl.ds(pl.multiple_of(i * TILE, TILE), TILE)
        ht_buf[cols, :] = h_buf[:, cols].T
        return carry

    lax.fori_loop(0, FF // TILE, turn_hidden, 0)
    local_in(2).wait()
    qs_buf[...] = split2(q_buf[...])

    def project(chip):
        rows = pl.ds(pl.multiple_of(chip * CHIP, CHIP), CHIP)
        proj[:, rows] = dot(qs_buf[...], g_buf[rows, :], (1, 1))

    def crossed(n):
        across(n, tensor, 0).wait_recv()

    crossed(0)
    crossed(1)
    project(z)
    for k in range(2):
        for way in range(2):
            own(way, k).wait_recv()
            if k == 0:
                onward(way).start()
            across(2 + 2 * k + way, (t_dn, t_up)[way], k if way == 0 else 1 - k).start()
    for n in range(2, 6):
        crossed(n)
    project(z_dn)
    project(z_up)
    for way in range(2):
        onward(way).wait_recv()
        across(6 + way, t_far, way).start()
    crossed(6)
    crossed(7)
    project(z_far)

    def grad_tiles(first, last):
        def body(m, carry):
            rows = pl.ds(pl.multiple_of(m * GRAD_TILE, GRAD_TILE), GRAD_TILE)
            for c in range(0, D, WIDTH):
                cols = pl.ds(c, WIDTH)
                grad_ref[rows, cols] = dot(ht_buf[rows, :], g_buf[:, cols], (1, 0))
            return carry

        lax.fori_loop(first, last, body, 0)

    def scatter(part, landing, peer, n):
        return pltpu.make_async_remote_copy(
            src_ref=part.at[peer], dst_ref=landing.at[dp], send_sem=sum_s.at[n],
            recv_sem=sum_r.at[n], device_id={"dp": peer}, device_id_type=MESH)

    def gather(total, peer, n):
        return pltpu.make_async_remote_copy(
            src_ref=total.at[dp], dst_ref=total.at[dp], send_sem=sum_s.at[n],
            recv_sem=sum_r.at[n], device_id={"dp": peer}, device_id_type=MESH)

    def wait_all(ref, sem):
        ref = ref.at[pl.ds(0, DP - 1)]
        pltpu.make_async_copy(ref, ref, sem).wait()

    power = join2(dot(split2(join2(proj[...])), h_buf[...], (1, 0)))
    for s in range(DP):
        if s < PSLICES:
            p_part[s] = power[:, s * PSLICE : (s + 1) * PSLICE]
        else:
            p_part[s] = jnp.zeros((RANK, PSLICE), F32)
    for peer in peers:
        scatter(p_part, p_in, peer, 0).start()
    p_in[dp] = p_part[dp]
    grad_tiles(0, FF // GRAD_TILE // 2)
    wait_all(p_in, sum_r.at[0])
    value = p_in[0]
    for s in range(1, DP):
        value = value + p_in[s]
    p_all[dp] = value
    for peer in peers:
        gather(p_all, peer, 1).start()
    grad_tiles(FF // GRAD_TILE // 2, FF // GRAD_TILE)
    wait_all(p_all, sum_r.at[1])

    power = jnp.concatenate([p_all[s] for s in range(PSLICES)], axis=1)
    gram = lax.dot_general(
        power, power, (((1,), (1,)), ((), ())), precision=HIGH, preferred_element_type=F32)
    gram_schmidt(gram, coeff)
    basis = jnp.dot(coeff[...], power, precision=HIGH, preferred_element_type=F32)
    p_ref[...] = basis

    basis2 = split2(basis)
    mapped = split2(join2(dot(basis2, ht_buf[...], (1, 0))))
    for c in range(0, D, WIDTH):
        terms = join2(dot(mapped, g_buf[:, c : c + WIDTH], (1, 0))).astype(BF16)
        for k in range(WIDTH // QSLICE):
            q_part[c // QSLICE + k] = terms[:, k * QSLICE : (k + 1) * QSLICE]
    for peer in peers:
        scatter(q_part, q_in, peer, 2).start()
    q_in[dp] = q_part[dp]
    p_turned_ref[...] = split2(p_ref[...]).T
    wait_all(q_in, sum_r.at[2])
    value = q_in[0].astype(F32)
    for s in range(1, DP):
        value = value + q_in[s].astype(F32)
    q_all[dp] = (value * (1.0 / DP)).astype(BF16)
    for peer in peers:
        gather(q_all, peer, 3).start()

    for way in range(2):
        for k in range(2):
            own(way, k).wait_send()
        onward(way).wait_send()
    for n in range(8):
        across(n, tensor, 0).wait_send()
    wait_all(p_part, sum_s.at[0])
    wait_all(p_all, sum_s.at[1])
    wait_all(q_part, sum_s.at[2])
    wait_all(q_all, sum_r.at[3])
    for s in range(DP):
        q_ref[:, s * QSLICE : (s + 1) * QSLICE] = q_all[s].astype(F32)
    wait_all(q_all, sum_s.at[3])


def error_kernel(
    grad_ref, p_ref, q_ref, p_turned_ref, p_out, q_out, error_out, q2, error_buf, sem, factor_sem
):
    factors = (
        pltpu.make_async_copy(p_ref, p_out, factor_sem.at[0]),
        pltpu.make_async_copy(q_ref, q_out, factor_sem.at[1]),
    )
    q_once = q_ref[...].astype(BF16)
    q2[...] = jnp.concatenate([q_once, q_once], axis=0)
    copies = []
    for m in range(FF // ERROR_TILE):
        rows = pl.ds(m * ERROR_TILE, ERROR_TILE)
        for c in range(0, D, ERROR_WIDTH):
            cols = pl.ds(c, ERROR_WIDTH)
            low_rank = dot(p_turned_ref[rows, :], q2[:, cols], (1, 0))
            error_buf[rows, cols] = (grad_ref[rows, cols] - low_rank).astype(BF16)
        copies.append(
            pltpu.make_async_copy(error_buf.at[rows], error_out.at[rows], sem.at[m]))
        copies[-1].start()
        if m == 0:
            for copy in factors:
                copy.start()
    for copy in copies:
        copy.wait()
    for copy in factors:
        copy.wait()


def on_device(gate_pre, up_pre, out_grad, q_start):
    hbm_in = [
        pltpu.with_memory_space_constraint(v, pltpu.HBM)
        for v in (gate_pre, up_pre, out_grad, q_start[0].T)
    ]
    any_space = pl.BlockSpec(memory_space=pl.ANY)
    vmem_space = pl.BlockSpec(memory_space=pltpu.VMEM)
    dma = pltpu.SemaphoreType.DMA
    grad, p_factor, q_factor, p_turned = pl.pallas_call(
        exchange_kernel,
        out_shape=(
            pltpu.VMEM((FF, D), F32),
            pltpu.VMEM((RANK, FF), F32),
            pltpu.VMEM((RANK, D), F32),
            pltpu.VMEM((FF, 2 * RANK), BF16),
        ),
        in_specs=[any_space] * 4,
        out_specs=(vmem_space,) * 4,
        scratch_shapes=[
            pltpu.VMEM((TOK, D), BF16),
            pltpu.VMEM((TOK, FF), BF16),
            pltpu.VMEM((TOK, FF), BF16),
            pltpu.VMEM((TOK, FF), BF16),
            pltpu.VMEM((FF, TOK), BF16),
            pltpu.VMEM((RANK, D), F32),
            pltpu.VMEM((2 * RANK, D), BF16),
            pltpu.VMEM((2 * RANK, TOK), F32),
            pltpu.VMEM((RANK, RANK), F32),
            pltpu.VMEM((DP, RANK, PSLICE), F32),
            pltpu.VMEM((DP, RANK, PSLICE), F32),
            pltpu.VMEM((DP, RANK, PSLICE), F32),
            pltpu.VMEM((DP, RANK, QSLICE), BF16),
            pltpu.VMEM((DP, RANK, QSLICE), BF16),
            pltpu.VMEM((DP, RANK, QSLICE), BF16),
            dma((5,)),
            dma((2, 2)), dma((2, 2)), dma((2,)), dma((2,)),
            dma((8,)), dma((8,)), dma((4,)), dma((4,)),
        ],
        compiler_params=pltpu.CompilerParams(
            collective_id=0, has_side_effects=True, vmem_limit_bytes=VMEM_BYTES),
        name="exchange",
    )(*hbm_in)
    p_out, q_out, new_error = pl.pallas_call(
        error_kernel,
        out_shape=(
            jax.ShapeDtypeStruct((RANK, FF), F32),
            jax.ShapeDtypeStruct((RANK, D), F32),
            jax.ShapeDtypeStruct((FF, D), BF16),
        ),
        in_specs=[vmem_space] * 4,
        out_specs=(any_space,) * 3,
        scratch_shapes=[
            pltpu.VMEM((2 * RANK, D), BF16),
            pltpu.VMEM((FF, D), BF16),
            dma((FF // ERROR_TILE,)),
            dma((2,)),
        ],
        compiler_params=pltpu.CompilerParams(vmem_limit_bytes=VMEM_BYTES),
        name="error",
    )(grad, p_factor, q_factor, p_turned)
    return (p_out.T, q_out.T[None], new_error[None])


def solution(mesh):
    placed = (
        P("dp", "tensor"),
        P("dp", "tensor"),
        P(("dp", "tensor"), None),
        P("tensor", None, None),
    )
    return jax.shard_map(
        on_device,
        mesh=mesh,
        in_specs=placed,
        out_specs=(P("tensor", None), P("tensor", None, None), P("dp", "tensor", None)),
        check_vma=False,
    )
```

time: 414 us -> 62.5 us (0.15)
  waiting for transfers between devices: 183 us -> 0 us
  matrix products: 123 us -> 0 us
  Pallas kernels: 0 us -> 61.3 us
  other arithmetic: 61 us -> 0 us
  between operations: 36.9 us -> 0.64 us
  local copies, waits for them, and re-layouts: 8.52 us -> 0 us
    psum x2 -> x0, waiting for transfers between devices: 144 us -> none  [the longest x1 83.6 us: on_device(): lax.psum(q_part.astype(jnp.bfloat16), 'dp').astype(jnp.float32) / replicas]
    dot_general x67 -> x0, matrix products: 123 us -> none  [the longest x1 30.6 us: on_device(): p_part = jnp.dot(gradient, q_local, precision=HIGH)]
    pallas_call x0 -> x2, Pallas kernels: none -> 61.3 us  [the longest x1 55.4 us: on_device(): pl.pallas_call(exchange_kernel, out_shape=(pltpu.VMEM((FF, D), F32), pltp...]
    another operation x62 -> x0, other arithmetic: 40.8 us -> none
    all_gather x1 -> x0, waiting for transfers between devices: 37.8 us -> none  [on_device(): full_grad = lax.all_gather(out_grad, 'tensor', axis=0, tiled=True)]
    reduce_sum x32 -> x0, other arithmetic: 19.3 us -> none  [orthonormal(): scaled = remainder * lax.rsqrt(jnp.sum(remainder * remainder) + epsilon)]
    scatter x32 -> x0, local copies, waits for them, and re-layouts: 5.82 us -> none  [orthonormal(): basis = basis.at[:, index].set(scaled)]
  transfers between devices with their start and end apart: 3 -> 0, of which waited for: 3 -> 0; matrix products, arithmetic and copies ran while one was open for 5% -> 0% of each run, Pallas kernels for 0% -> 0%
where the time goes in v2:
time: 62.5 us; the launch traced here: 62 us
  Pallas kernels  61.3 us (98%)
  between operations  0.64 us (1%)
    pallas_call x1, Pallas kernels, on_device(): pl.pallas_call(exchange_kernel, out_shape=(pltpu.VMEM((FF, D), F32), pltp...  55.4 us
    pallas_call x1, Pallas kernels, on_device(): pl.pallas_call(error_kernel, out_shape=(jax.ShapeDtypeStruct((RANK, FF),...  5.97 us

profile of v2, /device:TPU:1, one launch (start us, length us, event | category | flops | bytes accessed | tf_op | source)
XLA Modules:
  0.0 62.0 jit_solution(4969250438623770863)
XLA Ops:
  0.6 55.4 %exchange.1 = (f32[1792,4096]{1,0:T(8,128)S(1)}, f32[32,1792]{1,0:T(8,128)S(1)}, f32[32,4096]{1,0:T(8,128)S(1)}, bf16[1792,64]{1,0:T(8,128)(2,1)S(1)}) custom-call(bf16[512,1792]{1,0:T(8,128)(2,1)} %gate_hbm.1, bf16[512,1792]{1,0:T(8,128)(2,1)} %up_hbm.1, bf16[64,4096]{1,0:T(8,128)(2,1)} %out_grad_hbm.1, f32[32,4096]{1,0:T(8,128)} %bitcast.8), custom_call_target="tpu_custom_call" | custom-call | tf_op jit(solution)/shard_map/exchange/pallas_call | solution.py:338
  56.0 6.0 %error.1 = (f32[32,1792]{1,0:T(8,128)}, f32[32,4096]{1,0:T(8,128)}, bf16[1792,4096]{1,0:T(8,128)(2,1)}) custom-call(f32[1792,4096]{1,0:T(8,128)S(1)} %get-tuple-element.10.grad_ref, f32[32,1792]{1,0:T(8,128)S(1)} %get-tuple-element.11.p_ref, f32[32,4096]{1,0:T(8,128)S(1)} %get-tuple-element.12.q_ref, bf16[1792,64]{1,0:T(8,128)(2,1)S(1)} %get-tuple-element.13.p_turned_ref), custom_call_target="tpu_custom_call" | custom-call | tf_op jit(solution)/shard_map/error/pallas_call | solution.py:372

commit v3 on v2

--- a/solution.py
+++ b/solution.py
@@ -100,10 +100,10 @@
 
 def exchange_kernel(
     gate_hbm, up_hbm, out_grad_hbm, q_hbm,
-    grad_ref, p_ref, q_ref, p_turned_ref,
-    g_buf, gate_buf, up_buf, h_buf, ht_buf, q_buf, qs_buf, proj, coeff,
-    p_part, p_in, p_all, q_part, q_in, q_all,
-    local_sem, own_s, own_r, far_s, far_r, sib_s, sib_r, sum_s, sum_r,
+    grad_ref, p_ref, q_all, p_turned_ref,
+    g_buf, gate_buf, up_buf, h_buf, ht_buf, q_buf, qs_buf, proj_own, proj_out, proj_in, proj, coeff,
+    p_part, p_in, p_all, q_part, q_in,
+    local_sem, own_s, own_r, far_s, far_r, sib_s, sib_r, proj_s, proj_r, sum_s, sum_r, near_sem,
 ):
     dp = lax.axis_index("dp")
     tensor = lax.axis_index("tensor")
@@ -132,16 +132,28 @@
         src, dst = ((gate_hbm, gate_buf), (up_hbm, up_buf), (q_hbm, q_buf))[k]
         return pltpu.make_async_copy(src, dst, local_sem.at[2 + k])
 
+    near = [
+        y * 4 + lax.rem(x + 1, 4), y * 4 + lax.rem(x + 3, 4),
+        lax.rem(y + 1, 4) * 4 + x, lax.rem(y + 3, 4) * 4 + x,
+    ]
     barrier = pltpu.get_barrier_semaphore()
     for t in (t_up, t_dn, t_sib):
         pl.semaphore_signal(barrier, inc=1, device_id={"tensor": t}, device_id_type=MESH)
-    for peer in peers:
+    for peer in near:
         pl.semaphore_signal(barrier, inc=1, device_id={"dp": peer}, device_id_type=MESH)
     for h in range(2):
         local_g(h).start()
     for k in range(3):
         local_in(k).start()
-    pl.semaphore_wait(barrier, 3 + DP - 1)
+    pl.semaphore_wait(barrier, 3 + len(near))
+
+    def tell(n):
+        for peer in near:
+            pl.semaphore_signal(
+                near_sem.at[n], inc=1, device_id={"dp": peer}, device_id_type=MESH)
+
+    def hear(n):
+        pl.semaphore_wait(near_sem.at[n], len(near))
 
     def piece(t, h, to, send, recv):
         ref = g_buf.at[half_of(t, h), :]
@@ -166,6 +178,7 @@
             own(way, k).start()
     for h in range(2):
         across(h, tensor, h).start()
+    tell(0)
 
     local_in(0).wait()
     local_in(1).wait()
@@ -185,35 +198,51 @@
         return carry
 
     lax.fori_loop(0, FF // TILE, turn_hidden, 0)
-    local_in(2).wait()
-    qs_buf[...] = split2(q_buf[...])
-
-    def project(chip):
-        rows = pl.ds(pl.multiple_of(chip * CHIP, CHIP), CHIP)
-        proj[:, rows] = dot(qs_buf[...], g_buf[rows, :], (1, 1))
+    def q_across():
+        return pltpu.make_async_remote_copy(
+            src_ref=qs_buf.at[pl.ds(0, 2 * RANK)], dst_ref=qs_buf.at[pl.ds(2 * RANK, 2 * RANK)],
+            send_sem=proj_s.at[4], recv_sem=proj_r.at[4],
+            device_id={"tensor": t_sib}, device_id_type=MESH)
+
+    def proj_across(n):
+        return pltpu.make_async_remote_copy(
+            src_ref=proj_out.at[n], dst_ref=proj_in.at[n],
+            send_sem=proj_s.at[n], recv_sem=proj_r.at[n],
+            device_id={"tensor": t_sib}, device_id_type=MESH)
+
+    def project(n, t):
+        block = g_buf[pl.ds(pl.multiple_of(t * ROWS, ROWS), ROWS), :]
+        both = dot(qs_buf[...], jnp.concatenate([block, block], axis=0), (1, 1))
+        proj_own[n] = join2(both[: 2 * RANK])
+        proj_out[n] = join2(both[2 * RANK :])
+        proj_across(n).start()
 
     def crossed(n):
         across(n, tensor, 0).wait_recv()
 
-    crossed(0)
-    crossed(1)
-    project(z)
+    local_in(2).wait()
+    qs_buf[: 2 * RANK, :] = split2(q_buf[...])
+    q_across().start()
+    hear(0)
+    tell(1)
+    q_across().wait_recv()
+    project(0, tensor)
     for k in range(2):
         for way in range(2):
             own(way, k).wait_recv()
             if k == 0:
                 onward(way).start()
             across(2 + 2 * k + way, (t_dn, t_up)[way], k if way == 0 else 1 - k).start()
-    for n in range(2, 6):
-        crossed(n)
-    project(z_dn)
-    project(z_up)
+        if k == 0:
+            hear(1)
+            tell(2)
+    project(1, t_dn)
+    project(2, t_up)
+    hear(2)
     for way in range(2):
         onward(way).wait_recv()
         across(6 + way, t_far, way).start()
-    crossed(6)
-    crossed(7)
-    project(z_far)
+    project(3, t_far)
 
     def grad_tiles(first, last):
         def body(m, carry):
@@ -239,15 +268,26 @@
         ref = ref.at[pl.ds(0, DP - 1)]
         pltpu.make_async_copy(ref, ref, sem).wait()
 
-    power = join2(dot(split2(join2(proj[...])), h_buf[...], (1, 0)))
-    for s in range(DP):
-        if s < PSLICES:
-            p_part[s] = power[:, s * PSLICE : (s + 1) * PSLICE]
-        else:
-            p_part[s] = jnp.zeros((RANK, PSLICE), F32)
+    low_lanes = lax.broadcasted_iota(jnp.int32, (RANK, CHIP), 1) < ROWS
+    mine = jnp.logical_xor(low_lanes, core == 1)
+    for n, chip in enumerate((z, z_dn, z_up, z_far)):
+        proj_across(n).wait_recv()
+        cols = pl.ds(pl.multiple_of(chip * CHIP, CHIP), CHIP)
+        turned = jnp.where(mine, proj_own[n], proj_in[n])
+        proj[:, cols] = split2(turned)
+    projected = proj[...]
+
+    def p_slice(s):
+        s = jnp.minimum(s, PSLICES - 1)
+        cols = pl.ds(pl.multiple_of(s * PSLICE, PSLICE), PSLICE)
+        return join2(dot(projected, h_buf[:, cols], (1, 0)))
+
     for peer in peers:
+        p_part[peer] = p_slice(peer)
         scatter(p_part, p_in, peer, 0).start()
-    p_in[dp] = p_part[dp]
+    p_in[dp] = p_slice(dp)
+    for n in range(8):
+        crossed(n)
     grad_tiles(0, FF // GRAD_TILE // 2)
     wait_all(p_in, sum_r.at[0])
     value = p_in[0]
@@ -262,20 +302,22 @@
     power = jnp.concatenate([p_all[s] for s in range(PSLICES)], axis=1)
     gram = lax.dot_general(
         power, power, (((1,), (1,)), ((), ())), precision=HIGH, preferred_element_type=F32)
+    mapped_power = join2(dot(split2(power), ht_buf[...], (1, 0)))
     gram_schmidt(gram, coeff)
+    mapped = split2(
+        jnp.dot(coeff[...], mapped_power, precision=HIGH, preferred_element_type=F32))
+
+    def q_slice(s):
+        cols = pl.ds(pl.multiple_of(s * QSLICE, QSLICE), QSLICE)
+        return join2(dot(mapped, g_buf[:, cols], (1, 0))).astype(BF16)
+
+    for peer in peers:
+        q_part[peer] = q_slice(peer)
+        scatter(q_part, q_in, peer, 2).start()
+    q_in[dp] = q_slice(dp)
     basis = jnp.dot(coeff[...], power, precision=HIGH, preferred_element_type=F32)
     p_ref[...] = basis
-
-    basis2 = split2(basis)
-    mapped = split2(join2(dot(basis2, ht_buf[...], (1, 0))))
-    for c in range(0, D, WIDTH):
-        terms = join2(dot(mapped, g_buf[:, c : c + WIDTH], (1, 0))).astype(BF16)
-        for k in range(WIDTH // QSLICE):
-            q_part[c // QSLICE + k] = terms[:, k * QSLICE : (k + 1) * QSLICE]
-    for peer in peers:
-        scatter(q_part, q_in, peer, 2).start()
-    q_in[dp] = q_part[dp]
-    p_turned_ref[...] = split2(p_ref[...]).T
+    p_turned_ref[...] = split2(basis).T
     wait_all(q_in, sum_r.at[2])
     value = q_in[0].astype(F32)
     for s in range(1, DP):
@@ -290,24 +332,26 @@
         onward(way).wait_send()
     for n in range(8):
         across(n, tensor, 0).wait_send()
+    for n in range(4):
+        proj_across(n).wait_send()
+    q_across().wait_send()
     wait_all(p_part, sum_s.at[0])
     wait_all(p_all, sum_s.at[1])
     wait_all(q_part, sum_s.at[2])
+    wait_all(q_all, sum_s.at[3])
     wait_all(q_all, sum_r.at[3])
-    for s in range(DP):
-        q_ref[:, s * QSLICE : (s + 1) * QSLICE] = q_all[s].astype(F32)
-    wait_all(q_all, sum_s.at[3])
 
 
 def error_kernel(
-    grad_ref, p_ref, q_ref, p_turned_ref, p_out, q_out, error_out, q2, error_buf, sem, factor_sem
+    grad_ref, p_ref, q_ref, p_turned_ref, p_out, q_out, error_out,
+    q2, q_wide, error_buf, sem, factor_sem,
 ):
     factors = (
         pltpu.make_async_copy(p_ref, p_out, factor_sem.at[0]),
-        pltpu.make_async_copy(q_ref, q_out, factor_sem.at[1]),
+        pltpu.make_async_copy(q_wide, q_out, factor_sem.at[1]),
     )
-    q_once = q_ref[...].astype(BF16)
-    q2[...] = jnp.concatenate([q_once, q_once], axis=0)
+    for s in range(DP):
+        q2[:, s * QSLICE : (s + 1) * QSLICE] = jnp.concatenate([q_ref[s], q_ref[s]], axis=0)
     copies = []
     for m in range(FF // ERROR_TILE):
         rows = pl.ds(m * ERROR_TILE, ERROR_TILE)
@@ -319,6 +363,8 @@
             pltpu.make_async_copy(error_buf.at[rows], error_out.at[rows], sem.at[m]))
         copies[-1].start()
         if m == 0:
+            for s in range(DP):
+                q_wide[:, s * QSLICE : (s + 1) * QSLICE] = q_ref[s].astype(F32)
             for copy in factors:
                 copy.start()
     for copy in copies:
@@ -335,12 +381,12 @@
     any_space = pl.BlockSpec(memory_space=pl.ANY)
     vmem_space = pl.BlockSpec(memory_space=pltpu.VMEM)
     dma = pltpu.SemaphoreType.DMA
-    grad, p_factor, q_factor, p_turned = pl.pallas_call(
+    grad, p_factor, q_sums, p_turned = pl.pallas_call(
         exchange_kernel,
         out_shape=(
             pltpu.VMEM((FF, D), F32),
             pltpu.VMEM((RANK, FF), F32),
-            pltpu.VMEM((RANK, D), F32),
+            pltpu.VMEM((DP, RANK, QSLICE), BF16),
             pltpu.VMEM((FF, 2 * RANK), BF16),
         ),
         in_specs=[any_space] * 4,
@@ -352,18 +398,21 @@
             pltpu.VMEM((TOK, FF), BF16),
             pltpu.VMEM((FF, TOK), BF16),
             pltpu.VMEM((RANK, D), F32),
-            pltpu.VMEM((2 * RANK, D), BF16),
-            pltpu.VMEM((2 * RANK, TOK), F32),
+            pltpu.VMEM((4 * RANK, D), BF16),
+            pltpu.VMEM((4, RANK, CHIP), F32),
+            pltpu.VMEM((4, RANK, CHIP), F32),
+            pltpu.VMEM((4, RANK, CHIP), F32),
+            pltpu.VMEM((2 * RANK, TOK), BF16),
             pltpu.VMEM((RANK, RANK), F32),
             pltpu.VMEM((DP, RANK, PSLICE), F32),
             pltpu.VMEM((DP, RANK, PSLICE), F32),
             pltpu.VMEM((DP, RANK, PSLICE), F32),
             pltpu.VMEM((DP, RANK, QSLICE), BF16),
             pltpu.VMEM((DP, RANK, QSLICE), BF16),
-            pltpu.VMEM((DP, RANK, QSLICE), BF16),
             dma((5,)),
             dma((2, 2)), dma((2, 2)), dma((2,)), dma((2,)),
-            dma((8,)), dma((8,)), dma((4,)), dma((4,)),
+            dma((8,)), dma((8,)), dma((5,)), dma((5,)), dma((4,)), dma((4,)),
+            pltpu.SemaphoreType.REGULAR((3,)),
         ],
         compiler_params=pltpu.CompilerParams(
             collective_id=0, has_side_effects=True, vmem_limit_bytes=VMEM_BYTES),
@@ -380,13 +429,14 @@
         out_specs=(any_space,) * 3,
         scratch_shapes=[
             pltpu.VMEM((2 * RANK, D), BF16),
+            pltpu.VMEM((RANK, D), F32),
             pltpu.VMEM((FF, D), BF16),
             dma((FF // ERROR_TILE,)),
             dma((2,)),
         ],
         compiler_params=pltpu.CompilerParams(vmem_limit_bytes=VMEM_BYTES),
         name="error",
-    )(grad, p_factor, q_factor, p_turned)
+    )(grad, p_factor, q_sums, p_turned)
     return (p_out.T, q_out.T[None], new_error[None])
 
 

time: 62.5 us -> 61.3 us (0.981)
  Pallas kernels: 61.3 us -> 60.5 us
    pallas_call x1, Pallas kernels: 55.4 us -> 54.5 us  [on_device(): pl.pallas_call(exchange_kernel, out_shape=(pltpu.VMEM((FF, D), F32), pltp...]
where the time goes in v3:
time: 61.3 us; the launch traced here: 61.1 us
  Pallas kernels  60.5 us (99%)
  between operations  0.64 us (1%)
    pallas_call x1, Pallas kernels, on_device(): pl.pallas_call(exchange_kernel, out_shape=(pltpu.VMEM((FF, D), F32), pltp...  54.5 us
    pallas_call x1, Pallas kernels, on_device(): pl.pallas_call(error_kernel, out_shape=(jax.ShapeDtypeStruct((RANK, FF),...  5.97 us

profile of v3, /device:TPU:1, one launch (start us, length us, event | category | flops | bytes accessed | tf_op | source)
XLA Modules:
  0.0 61.1 jit_solution(1787854309798489971)
XLA Ops:
  0.6 54.5 %exchange.1 = (f32[1792,4096]{1,0:T(8,128)S(1)}, f32[32,1792]{1,0:T(8,128)S(1)}, bf16[16,32,256]{2,1,0:T(8,128)(2,1)S(1)}, bf16[1792,64]{1,0:T(8,128)(2,1)S(1)}) custom-call(bf16[512,1792]{1,0:T(8,128)(2,1)} %gate_hbm.1, bf16[512,1792]{1,0:T(8,128)(2,1)} %up_hbm.1, bf16[64,4096]{1,0:T(8,128)(2,1)} %out_grad_hbm.1, f32[32,4096]{1,0:T(8,128)} %bitcast.8), custom_call_target="tpu_custom_call" | custom-call | tf_op jit(solution)/shard_map/exchange/pallas_call | solution.py:384
  55.1 6.0 %error.1 = (f32[32,1792]{1,0:T(8,128)}, f32[32,4096]{1,0:T(8,128)}, bf16[1792,4096]{1,0:T(8,128)(2,1)}) custom-call(f32[1792,4096]{1,0:T(8,128)S(1)} %get-tuple-element.10.grad_ref, f32[32,1792]{1,0:T(8,128)S(1)} %get-tuple-element.11.p_ref, bf16[16,32,256]{2,1,0:T(8,128)(2,1)S(1)} %get-tuple-element.12.q_ref, ...), custom_call_target="tpu_custom_call" | custom-call | tf_op jit(solution)/shard_map/error/pallas_call | solution.py:421

commit v4 on v3

--- a/solution.py
+++ b/solution.py
@@ -20,6 +20,7 @@
 RANK = 32
 HALF = ROWS // 2
 CHIP = 2 * ROWS
+Q_HALF = 16
 DP = 16
 PSLICE = 128
 PSLICES = FF // PSLICE
@@ -101,9 +102,10 @@
 def exchange_kernel(
     gate_hbm, up_hbm, out_grad_hbm, q_hbm,
     grad_ref, p_ref, q_all, p_turned_ref,
-    g_buf, gate_buf, up_buf, h_buf, ht_buf, q_buf, qs_buf, proj_own, proj_out, proj_in, proj, coeff,
+    g_buf, gate_buf, up_buf, h_buf, ht_buf, q_buf, q_ring, proj_out, proj_in, proj, coeff,
     p_part, p_in, p_all, q_part, q_in,
-    local_sem, own_s, own_r, far_s, far_r, sib_s, sib_r, proj_s, proj_r, sum_s, sum_r, near_sem,
+    local_sem, q_own_s, q_own_r, q_far_s, q_far_r, own_s, own_r, far_s, far_r, sib_s, sib_r,
+    proj_s, proj_r, sum_s, sum_r, near_sem,
 ):
     dp = lax.axis_index("dp")
     tensor = lax.axis_index("tensor")
@@ -141,10 +143,13 @@
         pl.semaphore_signal(barrier, inc=1, device_id={"tensor": t}, device_id_type=MESH)
     for peer in near:
         pl.semaphore_signal(barrier, inc=1, device_id={"dp": peer}, device_id_type=MESH)
+    local_in(2).start()
     for h in range(2):
         local_g(h).start()
-    for k in range(3):
+    for k in range(2):
         local_in(k).start()
+    local_in(2).wait()
+    q_ring[z] = q_buf[...].astype(BF16)
     pl.semaphore_wait(barrier, 3 + len(near))
 
     def tell(n):
@@ -162,8 +167,12 @@
             device_id={"tensor": to}, device_id_type=MESH)
 
     def own(way, k):
-        h = k if way == 0 else 1 - k
-        return piece(tensor, h, (t_up, t_dn)[way], own_s.at[way, k], own_r.at[way, k])
+        h = (way, way, 1 - way)[k]
+        start, size = ((0, HALF // 2), (HALF // 2, HALF // 2), (0, HALF))[k]
+        ref = g_buf.at[pl.ds(pl.multiple_of(tensor * ROWS + h * HALF + start, HALF // 2), size), :]
+        return pltpu.make_async_remote_copy(
+            src_ref=ref, dst_ref=ref, send_sem=own_s.at[way, k], recv_sem=own_r.at[way, k],
+            device_id={"tensor": (t_up, t_dn)[way]}, device_id_type=MESH)
 
     def onward(way):
         return piece((t_dn, t_up)[way], way, (t_up, t_dn)[way], far_s.at[way], far_r.at[way])
@@ -171,14 +180,32 @@
     def across(n, t, h):
         return piece(t, h, t_sib, sib_s.at[n], sib_r.at[n])
 
+    def q_piece(chip, h, to, send, recv):
+        ref = q_ring.at[chip, pl.ds(h * Q_HALF, Q_HALF), :]
+        return pltpu.make_async_remote_copy(
+            src_ref=ref, dst_ref=ref, send_sem=send, recv_sem=recv,
+            device_id={"tensor": to}, device_id_type=MESH)
+
+    def q_own(way, k):
+        h = k if way == 0 else 1 - k
+        return q_piece(z, h, (t_up, t_dn)[way], q_own_s.at[way, k], q_own_r.at[way, k])
+
+    def q_onward(way):
+        return q_piece(
+            (z_dn, z_up)[way], way, (t_up, t_dn)[way], q_far_s.at[way], q_far_r.at[way])
+
+    for k in range(2):
+        for way in range(2):
+            q_own(way, k).start()
+    tell(0)
     for h in range(2):
         local_g(h).wait()
-    for k in range(2):
-        for way in range(2):
-            own(way, k).start()
-    for h in range(2):
         across(h, tensor, h).start()
-    tell(0)
+    for way in range(2):
+        q_own(way, 0).wait_recv()
+        q_onward(way).start()
+    for way in range(2):
+        own(way, 0).start()
 
     local_in(0).wait()
     local_in(1).wait()
@@ -198,51 +225,48 @@
         return carry
 
     lax.fori_loop(0, FF // TILE, turn_hidden, 0)
-    def q_across():
-        return pltpu.make_async_remote_copy(
-            src_ref=qs_buf.at[pl.ds(0, 2 * RANK)], dst_ref=qs_buf.at[pl.ds(2 * RANK, 2 * RANK)],
-            send_sem=proj_s.at[4], recv_sem=proj_r.at[4],
-            device_id={"tensor": t_sib}, device_id_type=MESH)
-
-    def proj_across(n):
-        return pltpu.make_async_remote_copy(
-            src_ref=proj_out.at[n], dst_ref=proj_in.at[n],
-            send_sem=proj_s.at[n], recv_sem=proj_r.at[n],
-            device_id={"tensor": t_sib}, device_id_type=MESH)
-
-    def project(n, t):
-        block = g_buf[pl.ds(pl.multiple_of(t * ROWS, ROWS), ROWS), :]
-        both = dot(qs_buf[...], jnp.concatenate([block, block], axis=0), (1, 1))
-        proj_own[n] = join2(both[: 2 * RANK])
-        proj_out[n] = join2(both[2 * RANK :])
-        proj_across(n).start()
+    chip_rows = pl.ds(pl.multiple_of(z * CHIP, CHIP), CHIP)
+
+    def project(chip):
+        return dot(q_ring[chip], g_buf[chip_rows, :], (1, 1))
+
+    def proj_send(n, to):
+        return pltpu.make_async_remote_copy(
+            src_ref=proj_out.at[n], dst_ref=proj_in.at[z], send_sem=proj_s.at[n],
+            recv_sem=proj_r.at[n], device_id={"tensor": to}, device_id_type=MESH)
 
     def crossed(n):
         across(n, tensor, 0).wait_recv()
 
-    local_in(2).wait()
-    qs_buf[: 2 * RANK, :] = split2(q_buf[...])
-    q_across().start()
+    def pass_on(k):
+        for way in range(2):
+            if k == 0:
+                own(way, 0).wait_recv()
+                own(way, 1).wait_recv()
+                onward(way).start()
+            else:
+                own(way, 2).wait_recv()
+            across(2 + 2 * k + way, (t_dn, t_up)[way], k if way == 0 else 1 - k).start()
+
     hear(0)
     tell(1)
-    q_across().wait_recv()
-    project(0, tensor)
-    for k in range(2):
+    crossed(0)
+    crossed(1)
+    proj_in[z] = project(z)
+    for way in range(2):
+        q_own(way, 1).wait_recv()
+    for n, (chip, to) in enumerate(((z_up, t_up), (z_dn, t_dn))):
+        proj_out[n] = project(chip)
+        proj_send(n, to).start()
+    for way in range(2):
+        q_onward(way).wait_recv()
+    proj_out[2] = project(z_far)
+    proj_send(2, t_far).start()
+    for k in (1, 2):
         for way in range(2):
-            own(way, k).wait_recv()
-            if k == 0:
-                onward(way).start()
-            across(2 + 2 * k + way, (t_dn, t_up)[way], k if way == 0 else 1 - k).start()
-        if k == 0:
-            hear(1)
-            tell(2)
-    project(1, t_dn)
-    project(2, t_up)
-    hear(2)
-    for way in range(2):
-        onward(way).wait_recv()
-        across(6 + way, t_far, way).start()
-    project(3, t_far)
+            own(way, k).start()
+    hear(1)
+    tell(2)
 
     def grad_tiles(first, last):
         def body(m, carry):
@@ -268,14 +292,13 @@
         ref = ref.at[pl.ds(0, DP - 1)]
         pltpu.make_async_copy(ref, ref, sem).wait()
 
-    low_lanes = lax.broadcasted_iota(jnp.int32, (RANK, CHIP), 1) < ROWS
-    mine = jnp.logical_xor(low_lanes, core == 1)
-    for n, chip in enumerate((z, z_dn, z_up, z_far)):
-        proj_across(n).wait_recv()
+    for n, (chip, to) in enumerate(((z_dn, t_up), (z_up, t_dn), (z_far, t_far), (z, None))):
+        if to is not None:
+            proj_send(n, to).wait_recv()
         cols = pl.ds(pl.multiple_of(chip * CHIP, CHIP), CHIP)
-        turned = jnp.where(mine, proj_own[n], proj_in[n])
-        proj[:, cols] = split2(turned)
+        proj[:, cols] = split2(proj_in[chip])
     projected = proj[...]
+    hear(2)
 
     def p_slice(s):
         s = jnp.minimum(s, PSLICES - 1)
@@ -286,9 +309,7 @@
         p_part[peer] = p_slice(peer)
         scatter(p_part, p_in, peer, 0).start()
     p_in[dp] = p_slice(dp)
-    for n in range(8):
-        crossed(n)
-    grad_tiles(0, FF // GRAD_TILE // 2)
+    pass_on(0)
     wait_all(p_in, sum_r.at[0])
     value = p_in[0]
     for s in range(1, DP):
@@ -296,7 +317,7 @@
     p_all[dp] = value
     for peer in peers:
         gather(p_all, peer, 1).start()
-    grad_tiles(FF // GRAD_TILE // 2, FF // GRAD_TILE)
+    pass_on(1)
     wait_all(p_all, sum_r.at[1])
 
     power = jnp.concatenate([p_all[s] for s in range(PSLICES)], axis=1)
@@ -307,6 +328,12 @@
     mapped = split2(
         jnp.dot(coeff[...], mapped_power, precision=HIGH, preferred_element_type=F32))
 
+    for way in range(2):
+        onward(way).wait_recv()
+        across(6 + way, t_far, way).start()
+    for n in range(2, 8):
+        crossed(n)
+
     def q_slice(s):
         cols = pl.ds(pl.multiple_of(s * QSLICE, QSLICE), QSLICE)
         return join2(dot(mapped, g_buf[:, cols], (1, 0))).astype(BF16)
@@ -315,9 +342,7 @@
         q_part[peer] = q_slice(peer)
         scatter(q_part, q_in, peer, 2).start()
     q_in[dp] = q_slice(dp)
-    basis = jnp.dot(coeff[...], power, precision=HIGH, preferred_element_type=F32)
-    p_ref[...] = basis
-    p_turned_ref[...] = split2(basis).T
+    grad_tiles(0, FF // GRAD_TILE // 2)
     wait_all(q_in, sum_r.at[2])
     value = q_in[0].astype(F32)
     for s in range(1, DP):
@@ -325,16 +350,22 @@
     q_all[dp] = (value * (1.0 / DP)).astype(BF16)
     for peer in peers:
         gather(q_all, peer, 3).start()
-
-    for way in range(2):
+    basis = jnp.dot(coeff[...], power, precision=HIGH, preferred_element_type=F32)
+    p_ref[...] = basis
+    p_turned_ref[...] = split2(basis).T
+    grad_tiles(FF // GRAD_TILE // 2, FF // GRAD_TILE)
+
+    for way in range(2):
+        for k in range(3):
+            own(way, k).wait_send()
         for k in range(2):
-            own(way, k).wait_send()
+            q_own(way, k).wait_send()
         onward(way).wait_send()
+        q_onward(way).wait_send()
     for n in range(8):
         across(n, tensor, 0).wait_send()
-    for n in range(4):
-        proj_across(n).wait_send()
-    q_across().wait_send()
+    for n in range(3):
+        proj_send(n, t_up).wait_send()
     wait_all(p_part, sum_s.at[0])
     wait_all(p_all, sum_s.at[1])
     wait_all(q_part, sum_s.at[2])
@@ -398,9 +429,8 @@
             pltpu.VMEM((TOK, FF), BF16),
             pltpu.VMEM((FF, TOK), BF16),
             pltpu.VMEM((RANK, D), F32),
-            pltpu.VMEM((4 * RANK, D), BF16),
-            pltpu.VMEM((4, RANK, CHIP), F32),
-            pltpu.VMEM((4, RANK, CHIP), F32),
+            pltpu.VMEM((4, RANK, D), BF16),
+            pltpu.VMEM((3, RANK, CHIP), F32),
             pltpu.VMEM((4, RANK, CHIP), F32),
             pltpu.VMEM((2 * RANK, TOK), BF16),
             pltpu.VMEM((RANK, RANK), F32),
@@ -411,7 +441,8 @@
             pltpu.VMEM((DP, RANK, QSLICE), BF16),
             dma((5,)),
             dma((2, 2)), dma((2, 2)), dma((2,)), dma((2,)),
-            dma((8,)), dma((8,)), dma((5,)), dma((5,)), dma((4,)), dma((4,)),
+            dma((2, 3)), dma((2, 3)), dma((2,)), dma((2,)),
+            dma((8,)), dma((8,)), dma((3,)), dma((3,)), dma((4,)), dma((4,)),
             pltpu.SemaphoreType.REGULAR((3,)),
         ],
         compiler_params=pltpu.CompilerParams(

time: 61.3 us -> 59.6 us (0.972)
  Pallas kernels: 60.5 us -> 58.9 us
    pallas_call x1, Pallas kernels: 54.5 us -> 52.9 us  [on_device(): pl.pallas_call(exchange_kernel, out_shape=(pltpu.VMEM((FF, D), F32), pltp...]
where the time goes in v4:
time: 59.6 us; the launch traced here: 59.5 us
  Pallas kernels  58.9 us (99%)
  between operations  0.64 us (1%)
    pallas_call x1, Pallas kernels, on_device(): pl.pallas_call(exchange_kernel, out_shape=(pltpu.VMEM((FF, D), F32), pltp...  52.9 us
    pallas_call x1, Pallas kernels, on_device(): pl.pallas_call(error_kernel, out_shape=(jax.ShapeDtypeStruct((RANK, FF),...  5.97 us

profile of v4, /device:TPU:1, one launch (start us, length us, event | category | flops | bytes accessed | tf_op | source)
XLA Modules:
  0.0 59.5 jit_solution(6440744417286334906)
XLA Ops:
  0.6 52.9 %exchange.1 = (f32[1792,4096]{1,0:T(8,128)S(1)}, f32[32,1792]{1,0:T(8,128)S(1)}, bf16[16,32,256]{2,1,0:T(8,128)(2,1)S(1)}, bf16[1792,64]{1,0:T(8,128)(2,1)S(1)}) custom-call(bf16[512,1792]{1,0:T(8,128)(2,1)} %gate_hbm.1, bf16[512,1792]{1,0:T(8,128)(2,1)} %up_hbm.1, bf16[64,4096]{1,0:T(8,128)(2,1)} %out_grad_hbm.1, f32[32,4096]{1,0:T(8,128)} %bitcast.8), custom_call_target="tpu_custom_call" | custom-call | tf_op jit(solution)/shard_map/exchange/pallas_call | solution.py:415
  53.5 6.0 %error.1 = (f32[32,1792]{1,0:T(8,128)}, f32[32,4096]{1,0:T(8,128)}, bf16[1792,4096]{1,0:T(8,128)(2,1)}) custom-call(f32[1792,4096]{1,0:T(8,128)S(1)} %get-tuple-element.10.grad_ref, f32[32,1792]{1,0:T(8,128)S(1)} %get-tuple-element.11.p_ref, bf16[16,32,256]{2,1,0:T(8,128)(2,1)S(1)} %get-tuple-element.12.q_ref, ...), custom_call_target="tpu_custom_call" | custom-call | tf_op jit(solution)/shard_map/error/pallas_call | solution.py:452

commit v5 on v4

--- a/solution.py
+++ b/solution.py
@@ -21,10 +21,14 @@
 HALF = ROWS // 2
 CHIP = 2 * ROWS
 Q_HALF = 16
+PART = HALF // 2
 DP = 16
 PSLICE = 128
 PSLICES = FF // PSLICE
 QSLICE = D // DP
+LINE = 4 * QSLICE
+RING = D - 2 * LINE
+EARLY = 2
 TILE = 256
 WIDTH = 512
 GRAD_TILE = 448
@@ -102,10 +106,10 @@
 def exchange_kernel(
     gate_hbm, up_hbm, out_grad_hbm, q_hbm,
     grad_ref, p_ref, q_all, p_turned_ref,
-    g_buf, gate_buf, up_buf, h_buf, ht_buf, q_buf, q_ring, proj_out, proj_in, proj, coeff,
+    g_buf, gate_buf, up_buf, h_buf, ht_buf, q_buf, q_ring, q_cross, proj_out, proj_in, proj, coeff,
     p_part, p_in, p_all, q_part, q_in,
-    local_sem, q_own_s, q_own_r, q_far_s, q_far_r, own_s, own_r, far_s, far_r, sib_s, sib_r,
-    proj_s, proj_r, sum_s, sum_r, near_sem,
+    local_sem, pull_s, pull_r, cross_s, cross_r, q_own_s, q_own_r, q_far_s, q_far_r, own_s, own_r, far_s, far_r,
+    sib_s, sib_r, far_sib_s, far_sib_r, proj_s, proj_r, sum_s, sum_r, near_sem,
 ):
     dp = lax.axis_index("dp")
     tensor = lax.axis_index("tensor")
@@ -116,11 +120,17 @@
     t_sib = z * 2 + 1 - core
     y = dp // 4
     x = lax.rem(dp, 4)
-    offsets = sorted(
-        ((a, b) for a in range(4) for b in range(4) if a or b),
-        key=lambda o: -(min(o[0], 4 - o[0]) + min(o[1], 4 - o[1])),
-    )
-    peers = [lax.rem(y + a, 4) * 4 + lax.rem(x + b, 4) for a, b in offsets]
+    hops = {
+        (a, b): min(a, 4 - a) + min(b, 4 - b) for a in range(4) for b in range(4) if a or b
+    }
+    peer_at = {
+        o: lax.rem(y + o[0], 4) * 4 + lax.rem(x + o[1], 4)
+        for o in sorted(hops, key=lambda o: -hops[o])
+    }
+    peers = list(peer_at.values())
+    near = [peer_at[o] for o in peer_at if hops[o] == 1]
+    opposite = [peer_at[0, 2], peer_at[2, 0]]
+    lines = ([peer_at[0, k] for k in (2, 1, 3)], [peer_at[k, 0] for k in (2, 1, 3)])
 
     def half_of(t, h):
         return pl.ds(pl.multiple_of(t * ROWS + h * HALF, HALF), HALF)
@@ -134,12 +144,8 @@
         src, dst = ((gate_hbm, gate_buf), (up_hbm, up_buf), (q_hbm, q_buf))[k]
         return pltpu.make_async_copy(src, dst, local_sem.at[2 + k])
 
-    near = [
-        y * 4 + lax.rem(x + 1, 4), y * 4 + lax.rem(x + 3, 4),
-        lax.rem(y + 1, 4) * 4 + x, lax.rem(y + 3, 4) * 4 + x,
-    ]
     barrier = pltpu.get_barrier_semaphore()
-    for t in (t_up, t_dn, t_sib):
+    for t in (t_up, t_dn, t_far, t_sib):
         pl.semaphore_signal(barrier, inc=1, device_id={"tensor": t}, device_id_type=MESH)
     for peer in near:
         pl.semaphore_signal(barrier, inc=1, device_id={"dp": peer}, device_id_type=MESH)
@@ -149,16 +155,37 @@
     for k in range(2):
         local_in(k).start()
     local_in(2).wait()
-    q_ring[z] = q_buf[...].astype(BF16)
-    pl.semaphore_wait(barrier, 3 + len(near))
+    q_ring[0] = q_buf[:, :RING].astype(BF16)
+    for line in range(2):
+        for k in range(4):
+            col = RING + line * LINE + k * QSLICE
+            q_cross[line, k, 0] = q_buf[:, col : col + QSLICE].astype(BF16)
+    pl.semaphore_wait(barrier, 4 + len(near))
 
     def tell(n):
-        for peer in near:
+        for peer in (near, opposite)[n]:
             pl.semaphore_signal(
                 near_sem.at[n], inc=1, device_id={"dp": peer}, device_id_type=MESH)
 
     def hear(n):
-        pl.semaphore_wait(near_sem.at[n], len(near))
+        pl.semaphore_wait(near_sem.at[n], (len(near), len(opposite))[n])
+
+    def pull(n, line):
+        to, place = ((t_up, 3), (t_dn, 1), (t_far, 2))[n]
+        part = q_cross.at[line, (x, y)[line]]
+        return pltpu.make_async_remote_copy(
+            src_ref=part.at[0], dst_ref=part.at[place], send_sem=pull_s.at[n, line],
+            recv_sem=pull_r.at[n, line], device_id={"tensor": to}, device_id_type=MESH)
+
+    def spread(line, peer):
+        ref = q_cross.at[line, (x, y)[line], pl.ds(1, 3)]
+        return pltpu.make_async_remote_copy(
+            src_ref=ref, dst_ref=ref, send_sem=cross_s.at[line], recv_sem=cross_r.at[line],
+            device_id={"dp": peer}, device_id_type=MESH)
+
+    def spread_wait(line, sem):
+        ref = q_cross.at[line, pl.ds(0, 3), pl.ds(1, 3)]
+        pltpu.make_async_copy(ref, ref, sem.at[line]).wait()
 
     def piece(t, h, to, send, recv):
         ref = g_buf.at[half_of(t, h), :]
@@ -166,34 +193,52 @@
             src_ref=ref, dst_ref=ref, send_sem=send, recv_sem=recv,
             device_id={"tensor": to}, device_id_type=MESH)
 
+    pieces = ((0, PART, 0, D // 2), (0, PART, D // 2, D // 2), (PART, PART, 0, D), (0, HALF, 0, D))
+
     def own(way, k):
-        h = (way, way, 1 - way)[k]
-        start, size = ((0, HALF // 2), (HALF // 2, HALF // 2), (0, HALF))[k]
-        ref = g_buf.at[pl.ds(pl.multiple_of(tensor * ROWS + h * HALF + start, HALF // 2), size), :]
+        h = 1 - way if k == 3 else way
+        row, rows, col, cols = pieces[k]
+        ref = g_buf.at[
+            pl.ds(pl.multiple_of(tensor * ROWS + h * HALF + row, PART), rows), pl.ds(col, cols)]
         return pltpu.make_async_remote_copy(
             src_ref=ref, dst_ref=ref, send_sem=own_s.at[way, k], recv_sem=own_r.at[way, k],
             device_id={"tensor": (t_up, t_dn)[way]}, device_id_type=MESH)
 
-    def onward(way):
-        return piece((t_dn, t_up)[way], way, (t_up, t_dn)[way], far_s.at[way], far_r.at[way])
+    def part_of(t, h, part):
+        return g_buf.at[pl.ds(pl.multiple_of(t * ROWS + h * HALF + part * PART, PART), PART), :]
+
+    def onward(way, part):
+        ref = part_of((t_dn, t_up)[way], way, part)
+        return pltpu.make_async_remote_copy(
+            src_ref=ref, dst_ref=ref, send_sem=far_s.at[way, part], recv_sem=far_r.at[way, part],
+            device_id={"tensor": (t_up, t_dn)[way]}, device_id_type=MESH)
+
+    def far_across(way, part):
+        ref = part_of(t_far, way, part)
+        return pltpu.make_async_remote_copy(
+            src_ref=ref, dst_ref=ref, send_sem=far_sib_s.at[way, part],
+            recv_sem=far_sib_r.at[way, part], device_id={"tensor": t_sib}, device_id_type=MESH)
 
     def across(n, t, h):
         return piece(t, h, t_sib, sib_s.at[n], sib_r.at[n])
 
-    def q_piece(chip, h, to, send, recv):
-        ref = q_ring.at[chip, pl.ds(h * Q_HALF, Q_HALF), :]
-        return pltpu.make_async_remote_copy(
-            src_ref=ref, dst_ref=ref, send_sem=send, recv_sem=recv,
-            device_id={"tensor": to}, device_id_type=MESH)
+    def q_piece(source, place, h, to, send, recv):
+        rows = pl.ds(h * Q_HALF, Q_HALF)
+        return pltpu.make_async_remote_copy(
+            src_ref=q_ring.at[source, rows, :], dst_ref=q_ring.at[place, rows, :],
+            send_sem=send, recv_sem=recv, device_id={"tensor": to}, device_id_type=MESH)
 
     def q_own(way, k):
         h = k if way == 0 else 1 - k
-        return q_piece(z, h, (t_up, t_dn)[way], q_own_s.at[way, k], q_own_r.at[way, k])
+        return q_piece(
+            0, (3, 1)[way], h, (t_up, t_dn)[way], q_own_s.at[way, k], q_own_r.at[way, k])
 
     def q_onward(way):
-        return q_piece(
-            (z_dn, z_up)[way], way, (t_up, t_dn)[way], q_far_s.at[way], q_far_r.at[way])
-
+        return q_piece((3, 1)[way], 2, way, (t_up, t_dn)[way], q_far_s.at[way], q_far_r.at[way])
+
+    for n in range(3):
+        for line in range(2):
+            pull(n, line).start()
     for k in range(2):
         for way in range(2):
             q_own(way, k).start()
@@ -201,11 +246,19 @@
     for h in range(2):
         local_g(h).wait()
         across(h, tensor, h).start()
+    hear(0)
+    tell(1)
+    for line in range(2):
+        for n in range(3):
+            pull(n, line).wait_recv()
+        for peer in lines[line]:
+            spread(line, peer).start()
     for way in range(2):
         q_own(way, 0).wait_recv()
         q_onward(way).start()
-    for way in range(2):
-        own(way, 0).start()
+    for k in range(EARLY):
+        for way in range(2):
+            own(way, k).start()
 
     local_in(0).wait()
     local_in(1).wait()
@@ -227,9 +280,6 @@
     lax.fori_loop(0, FF // TILE, turn_hidden, 0)
     chip_rows = pl.ds(pl.multiple_of(z * CHIP, CHIP), CHIP)
 
-    def project(chip):
-        return dot(q_ring[chip], g_buf[chip_rows, :], (1, 1))
-
     def proj_send(n, to):
         return pltpu.make_async_remote_copy(
             src_ref=proj_out.at[n], dst_ref=proj_in.at[z], send_sem=proj_s.at[n],
@@ -243,30 +293,38 @@
             if k == 0:
                 own(way, 0).wait_recv()
                 own(way, 1).wait_recv()
-                onward(way).start()
+                onward(way, 0).start()
             else:
+                own(way, 3).wait_recv()
+                across(4 + way, (t_dn, t_up)[way], 1 - way).start()
+        if k == 0:
+            for way in range(2):
                 own(way, 2).wait_recv()
-            across(2 + 2 * k + way, (t_dn, t_up)[way], k if way == 0 else 1 - k).start()
-
-    hear(0)
-    tell(1)
+                onward(way, 1).start()
+                across(2 + way, (t_dn, t_up)[way], way).start()
+
     crossed(0)
     crossed(1)
-    proj_in[z] = project(z)
     for way in range(2):
         q_own(way, 1).wait_recv()
-    for n, (chip, to) in enumerate(((z_up, t_up), (z_dn, t_dn))):
-        proj_out[n] = project(chip)
+        q_onward(way).wait_recv()
+    results = dot(q_ring[...].reshape(4 * RANK, RING), g_buf[chip_rows, :RING], (1, 1))
+    for line in range(2):
+        spread_wait(line, cross_r)
+        for k in range(4):
+            col = RING + line * LINE + k * QSLICE
+            results += dot(
+                q_cross[line, k].reshape(4 * RANK, QSLICE), g_buf[chip_rows, col : col + QSLICE],
+                (1, 1))
+    proj_in[z] = results[:RANK]
+    for n, (place, to) in enumerate(((1, t_up), (3, t_dn), (2, t_far))):
+        proj_out[n] = results[place * RANK : (place + 1) * RANK]
+    for n, to in ((2, t_far), (0, t_up), (1, t_dn)):
         proj_send(n, to).start()
-    for way in range(2):
-        q_onward(way).wait_recv()
-    proj_out[2] = project(z_far)
-    proj_send(2, t_far).start()
-    for k in (1, 2):
+    for k in range(EARLY, 4):
         for way in range(2):
             own(way, k).start()
     hear(1)
-    tell(2)
 
     def grad_tiles(first, last):
         def body(m, carry):
@@ -298,7 +356,6 @@
         cols = pl.ds(pl.multiple_of(chip * CHIP, CHIP), CHIP)
         proj[:, cols] = split2(proj_in[chip])
     projected = proj[...]
-    hear(2)
 
     def p_slice(s):
         s = jnp.minimum(s, PSLICES - 1)
@@ -328,11 +385,18 @@
     mapped = split2(
         jnp.dot(coeff[...], mapped_power, precision=HIGH, preferred_element_type=F32))
 
-    for way in range(2):
-        onward(way).wait_recv()
-        across(6 + way, t_far, way).start()
-    for n in range(2, 8):
+    basis = jnp.dot(coeff[...], power, precision=HIGH, preferred_element_type=F32)
+    p_ref[...] = basis
+    p_turned_ref[...] = split2(basis).T
+    for part in range(2):
+        for way in range(2):
+            onward(way, part).wait_recv()
+            far_across(way, part).start()
+    for n in range(2, 6):
         crossed(n)
+    for part in range(2):
+        for way in range(2):
+            far_across(way, part).wait_recv()
 
     def q_slice(s):
         cols = pl.ds(pl.multiple_of(s * QSLICE, QSLICE), QSLICE)
@@ -350,22 +414,24 @@
     q_all[dp] = (value * (1.0 / DP)).astype(BF16)
     for peer in peers:
         gather(q_all, peer, 3).start()
-    basis = jnp.dot(coeff[...], power, precision=HIGH, preferred_element_type=F32)
-    p_ref[...] = basis
-    p_turned_ref[...] = split2(basis).T
     grad_tiles(FF // GRAD_TILE // 2, FF // GRAD_TILE)
 
     for way in range(2):
-        for k in range(3):
+        for k in range(4):
             own(way, k).wait_send()
         for k in range(2):
             q_own(way, k).wait_send()
-        onward(way).wait_send()
+            onward(way, k).wait_send()
+            far_across(way, k).wait_send()
         q_onward(way).wait_send()
-    for n in range(8):
+    for n in range(6):
         across(n, tensor, 0).wait_send()
     for n in range(3):
         proj_send(n, t_up).wait_send()
+        for line in range(2):
+            pull(n, line).wait_send()
+    for line in range(2):
+        spread_wait(line, cross_s)
     wait_all(p_part, sum_s.at[0])
     wait_all(p_all, sum_s.at[1])
     wait_all(q_part, sum_s.at[2])
@@ -429,7 +495,8 @@
             pltpu.VMEM((TOK, FF), BF16),
             pltpu.VMEM((FF, TOK), BF16),
             pltpu.VMEM((RANK, D), F32),
-            pltpu.VMEM((4, RANK, D), BF16),
+            pltpu.VMEM((4, RANK, RING), BF16),
+            pltpu.VMEM((2, 4, 4, RANK, QSLICE), BF16),
             pltpu.VMEM((3, RANK, CHIP), F32),
             pltpu.VMEM((4, RANK, CHIP), F32),
             pltpu.VMEM((2 * RANK, TOK), BF16),
@@ -440,10 +507,12 @@
             pltpu.VMEM((DP, RANK, QSLICE), BF16),
             pltpu.VMEM((DP, RANK, QSLICE), BF16),
             dma((5,)),
+            dma((3, 2)), dma((3, 2)), dma((2,)), dma((2,)),
             dma((2, 2)), dma((2, 2)), dma((2,)), dma((2,)),
-            dma((2, 3)), dma((2, 3)), dma((2,)), dma((2,)),
-            dma((8,)), dma((8,)), dma((3,)), dma((3,)), dma((4,)), dma((4,)),
-            pltpu.SemaphoreType.REGULAR((3,)),
+            dma((2, 4)), dma((2, 4)), dma((2, 2)), dma((2, 2)),
+            dma((6,)), dma((6,)), dma((2, 2)), dma((2, 2)),
+            dma((3,)), dma((3,)), dma((4,)), dma((4,)),
+            pltpu.SemaphoreType.REGULAR((2,)),
         ],
         compiler_params=pltpu.CompilerParams(
             collective_id=0, has_side_effects=True, vmem_limit_bytes=VMEM_BYTES),

time: 59.6 us -> 58.1 us (0.975)
  Pallas kernels: 58.9 us -> 57.3 us
    pallas_call x1, Pallas kernels: 52.9 us -> 51.4 us  [on_device(): pl.pallas_call(exchange_kernel, out_shape=(pltpu.VMEM((FF, D), F32), pltp...]
where the time goes in v5:
time: 58.1 us; the launch traced here: 58 us
  Pallas kernels  57.3 us (99%)
  between operations  0.64 us (1%)
    pallas_call x1, Pallas kernels, on_device(): pl.pallas_call(exchange_kernel, out_shape=(pltpu.VMEM((FF, D), F32), pltp...  51.4 us
    pallas_call x1, Pallas kernels, on_device(): pl.pallas_call(error_kernel, out_shape=(jax.ShapeDtypeStruct((RANK, FF),...  5.97 us

profile of v5, /device:TPU:1, one launch (start us, length us, event | category | flops | bytes accessed | tf_op | source)
XLA Modules:
  0.0 58.0 jit_solution(17315233563773025563)
XLA Ops:
  0.6 51.4 %exchange.1 = (f32[1792,4096]{1,0:T(8,128)S(1)}, f32[32,1792]{1,0:T(8,128)S(1)}, bf16[16,32,256]{2,1,0:T(8,128)(2,1)S(1)}, bf16[1792,64]{1,0:T(8,128)(2,1)S(1)}) custom-call(bf16[512,1792]{1,0:T(8,128)(2,1)} %gate_hbm.1, bf16[512,1792]{1,0:T(8,128)(2,1)} %up_hbm.1, bf16[64,4096]{1,0:T(8,128)(2,1)} %out_grad_hbm.1, f32[32,4096]{1,0:T(8,128)} %bitcast.8), custom_call_target="tpu_custom_call" | custom-call | tf_op jit(solution)/shard_map/exchange/pallas_call | solution.py:481
  52.0 6.0 %error.1 = (f32[32,1792]{1,0:T(8,128)}, f32[32,4096]{1,0:T(8,128)}, bf16[1792,4096]{1,0:T(8,128)(2,1)}) custom-call(f32[1792,4096]{1,0:T(8,128)S(1)} %get-tuple-element.10.grad_ref, f32[32,1792]{1,0:T(8,128)S(1)} %get-tuple-element.11.p_ref, bf16[16,32,256]{2,1,0:T(8,128)(2,1)S(1)} %get-tuple-element.12.q_ref, ...), custom_call_target="tpu_custom_call" | custom-call | tf_op jit(solution)/shard_map/error/pallas_call | solution.py:521

commit v6 on v5

--- a/solution.py
+++ b/solution.py
@@ -363,21 +363,21 @@
         return join2(dot(projected, h_buf[:, cols], (1, 0)))
 
     for peer in peers:
-        p_part[peer] = p_slice(peer)
+        p_part[peer] = p_slice(peer).astype(BF16)
         scatter(p_part, p_in, peer, 0).start()
-    p_in[dp] = p_slice(dp)
+    p_in[dp] = p_slice(dp).astype(BF16)
     pass_on(0)
     wait_all(p_in, sum_r.at[0])
-    value = p_in[0]
+    value = p_in[0].astype(F32)
     for s in range(1, DP):
-        value = value + p_in[s]
-    p_all[dp] = value
+        value = value + p_in[s].astype(F32)
+    p_all[dp] = value.astype(BF16)
     for peer in peers:
         gather(p_all, peer, 1).start()
     pass_on(1)
     wait_all(p_all, sum_r.at[1])
 
-    power = jnp.concatenate([p_all[s] for s in range(PSLICES)], axis=1)
+    power = jnp.concatenate([p_all[s] for s in range(PSLICES)], axis=1).astype(F32)
     gram = lax.dot_general(
         power, power, (((1,), (1,)), ((), ())), precision=HIGH, preferred_element_type=F32)
     mapped_power = join2(dot(split2(power), ht_buf[...], (1, 0)))
@@ -501,9 +501,9 @@
             pltpu.VMEM((4, RANK, CHIP), F32),
             pltpu.VMEM((2 * RANK, TOK), BF16),
             pltpu.VMEM((RANK, RANK), F32),
-            pltpu.VMEM((DP, RANK, PSLICE), F32),
-            pltpu.VMEM((DP, RANK, PSLICE), F32),
-            pltpu.VMEM((DP, RANK, PSLICE), F32),
+            pltpu.VMEM((DP, RANK, PSLICE), BF16),
+            pltpu.VMEM((DP, RANK, PSLICE), BF16),
+            pltpu.VMEM((DP, RANK, PSLICE), BF16),
             pltpu.VMEM((DP, RANK, QSLICE), BF16),
             pltpu.VMEM((DP, RANK, QSLICE), BF16),
             dma((5,)),

time: 58.1 us -> 56.2 us (0.967)
  Pallas kernels: 57.3 us -> 55.5 us
    pallas_call x1, Pallas kernels: 51.4 us -> 49.5 us  [on_device(): pl.pallas_call(exchange_kernel, out_shape=(pltpu.VMEM((FF, D), F32), pltp...]
where the time goes in v6:
time: 56.2 us; the launch traced here: 56.1 us
  Pallas kernels  55.5 us (99%)
  between operations  0.64 us (1%)
    pallas_call x1, Pallas kernels, on_device(): pl.pallas_call(exchange_kernel, out_shape=(pltpu.VMEM((FF, D), F32), pltp...  49.5 us
    pallas_call x1, Pallas kernels, on_device(): pl.pallas_call(error_kernel, out_shape=(jax.ShapeDtypeStruct((RANK, FF),...  5.97 us

profile of v6, /device:TPU:1, one launch (start us, length us, event | category | flops | bytes accessed | tf_op | source)
XLA Modules:
  0.0 56.1 jit_solution(14695510657036468816)
XLA Ops:
  0.6 49.5 %exchange.1 = (f32[1792,4096]{1,0:T(8,128)S(1)}, f32[32,1792]{1,0:T(8,128)S(1)}, bf16[16,32,256]{2,1,0:T(8,128)(2,1)S(1)}, bf16[1792,64]{1,0:T(8,128)(2,1)S(1)}) custom-call(bf16[512,1792]{1,0:T(8,128)(2,1)} %gate_hbm.1, bf16[512,1792]{1,0:T(8,128)(2,1)} %up_hbm.1, bf16[64,4096]{1,0:T(8,128)(2,1)} %out_grad_hbm.1, f32[32,4096]{1,0:T(8,128)} %bitcast.8), custom_call_target="tpu_custom_call" | custom-call | tf_op jit(solution)/shard_map/exchange/pallas_call | solution.py:481
  50.1 6.0 %error.1 = (f32[32,1792]{1,0:T(8,128)}, f32[32,4096]{1,0:T(8,128)}, bf16[1792,4096]{1,0:T(8,128)(2,1)}) custom-call(f32[1792,4096]{1,0:T(8,128)S(1)} %get-tuple-element.10.grad_ref, f32[32,1792]{1,0:T(8,128)S(1)} %get-tuple-element.11.p_ref, bf16[16,32,256]{2,1,0:T(8,128)(2,1)S(1)} %get-tuple-element.12.q_ref, ...), custom_call_target="tpu_custom_call" | custom-call | tf_op jit(solution)/shard_map/error/pallas_call | solution.py:521

commit v7 on v6

--- a/solution.py
+++ b/solution.py
@@ -362,9 +362,11 @@
         cols = pl.ds(pl.multiple_of(s * PSLICE, PSLICE), PSLICE)
         return join2(dot(projected, h_buf[:, cols], (1, 0)))
 
-    for peer in peers:
-        p_part[peer] = p_slice(peer).astype(BF16)
-        scatter(p_part, p_in, peer, 0).start()
+    for first in range(0, len(peers), 5):
+        for peer in peers[first : first + 5]:
+            p_part[peer] = p_slice(peer).astype(BF16)
+        for peer in peers[first : first + 5]:
+            scatter(p_part, p_in, peer, 0).start()
     p_in[dp] = p_slice(dp).astype(BF16)
     pass_on(0)
     wait_all(p_in, sum_r.at[0])
@@ -402,9 +404,11 @@
         cols = pl.ds(pl.multiple_of(s * QSLICE, QSLICE), QSLICE)
         return join2(dot(mapped, g_buf[:, cols], (1, 0))).astype(BF16)
 
-    for peer in peers:
-        q_part[peer] = q_slice(peer)
-        scatter(q_part, q_in, peer, 2).start()
+    for first in range(0, len(peers), 5):
+        for peer in peers[first : first + 5]:
+            q_part[peer] = q_slice(peer)
+        for peer in peers[first : first + 5]:
+            scatter(q_part, q_in, peer, 2).start()
     q_in[dp] = q_slice(dp)
     grad_tiles(0, FF // GRAD_TILE // 2)
     wait_all(q_in, sum_r.at[2])

time: 56.2 us -> 54 us (0.961)
  Pallas kernels: 55.5 us -> 53.2 us
    pallas_call x1, Pallas kernels: 49.5 us -> 47.3 us  [on_device(): pl.pallas_call(exchange_kernel, out_shape=(pltpu.VMEM((FF, D), F32), pltp...]
where the time goes in v7:
time: 54 us; the launch traced here: 53.9 us
  Pallas kernels  53.2 us (99%)
  between operations  0.64 us (1%)
    pallas_call x1, Pallas kernels, on_device(): pl.pallas_call(exchange_kernel, out_shape=(pltpu.VMEM((FF, D), F32), pltp...  47.3 us
    pallas_call x1, Pallas kernels, on_device(): pl.pallas_call(error_kernel, out_shape=(jax.ShapeDtypeStruct((RANK, FF),...  5.97 us

profile of v7, /device:TPU:1, one launch (start us, length us, event | category | flops | bytes accessed | tf_op | source)
XLA Modules:
  0.0 53.9 jit_solution(7965985292872945897)
XLA Ops:
  0.6 47.3 %exchange.1 = (f32[1792,4096]{1,0:T(8,128)S(1)}, f32[32,1792]{1,0:T(8,128)S(1)}, bf16[16,32,256]{2,1,0:T(8,128)(2,1)S(1)}, bf16[1792,64]{1,0:T(8,128)(2,1)S(1)}) custom-call(bf16[512,1792]{1,0:T(8,128)(2,1)} %gate_hbm.1, bf16[512,1792]{1,0:T(8,128)(2,1)} %up_hbm.1, bf16[64,4096]{1,0:T(8,128)(2,1)} %out_grad_hbm.1, f32[32,4096]{1,0:T(8,128)} %bitcast.8), custom_call_target="tpu_custom_call" | custom-call | tf_op jit(solution)/shard_map/exchange/pallas_call | solution.py:485
  47.9 6.0 %error.1 = (f32[32,1792]{1,0:T(8,128)}, f32[32,4096]{1,0:T(8,128)}, bf16[1792,4096]{1,0:T(8,128)(2,1)}) custom-call(f32[1792,4096]{1,0:T(8,128)S(1)} %get-tuple-element.10.grad_ref, f32[32,1792]{1,0:T(8,128)S(1)} %get-tuple-element.11.p_ref, bf16[16,32,256]{2,1,0:T(8,128)(2,1)S(1)} %get-tuple-element.12.q_ref, ...), custom_call_target="tpu_custom_call" | custom-call | tf_op jit(solution)/shard_map/error/pallas_call | solution.py:525
